TPU v7x, 512 devices: a whole 4x8x8 slice. The times are simulated.
512 devices in a mesh: patch: 128 (over y, z, core), pair: 4 (over x).
Axes of the slice: x: 4, y: 8, z: 8, core: 2. Of those that a mesh axis runs over, the one named last changes fastest.
Arguments:
- right_side: float32 [262144], P('patch'), may hold values from -8 to 8
- coords: float32 [3, 262144], P(None, 'patch'), as said below
- diagonal: float32 [262144], P('patch'), may hold values from 1 to 2
- near_pairs: int32 [2, 8192], P(None, ('patch', 'pair')), may hold values from 0 to 1023, as said below
- far_pairs: int32 [2, 16384], P(None, ('patch', 'pair')), may hold values from 0 to 1023, as said below
- far_rank: int32 [16384], P(('patch', 'pair')), may hold values from 1 to 32, as said below
- far_left: bfloat16 [16384, 32, 256], P(('patch', 'pair')), may hold values from -0.375 to 0.375
- far_right: bfloat16 [16384, 32, 256], P(('patch', 'pair')), may hold values from -0.375 to 0.375
- far_scale: float32 [16384, 32], P(('patch', 'pair')), may hold values from 0.02 to 0.3
Outputs:
- solution: float32 [262144], P('patch')
- residual_norm: float32 [], replicated
Inputs may be any that keep to these rules, and one draw needn't show every extreme that they name: Column k of near_pairs belongs to patch group g = k // 64; its target block lies among blocks g*8 to (g+1)*8 - 1, its source differs from the target by 1 to 4 blocks, and 4 is reached on every device. Column k of far_pairs belongs to patch group g = k // 128; its target block lies among that group's blocks, its source lies more than 4 blocks from the target, anywhere else. `far_rank`: every device holds a far pair of rank 32. `coords`: panel centres of block b lie within distance 2 in each component of (b / 2, 0.3 sin(0.7 b), 0).
All inputs are finite; a program needn't handle non-finite values.
Results may differ from a plain program's by a relative error of at most 0.0003.
Values sent between devices are 32-bit elements; how exact they have to be, the bound alone decides.
A program may use at most 64 MiB of HBM per device.

v0:
```python
import jax
import jax.numpy as jnp
from jax import lax
from jax.sharding import PartitionSpec as P

BS = 256
ITERS = 2
BLK_DEV = 8
RIM = 4


NEAR_GAIN = 2.0
SOFT_SQ = 0.25
HIGH = lax.Precision.HIGHEST


def with_halo(block, sides, width):
    for axis, dim in sides:
        count = lax.axis_size(axis)
        forward = [(i, i + 1) for i in range(count - 1)]
        backward = [(target, source) for source, target in forward]
        low = lax.ppermute(
            lax.slice_in_dim(block, block.shape[dim] - width, None, axis=dim), axis, forward
        )
        high = lax.ppermute(lax.slice_in_dim(block, 0, width, axis=dim), axis, backward)
        block = jnp.concatenate([low, block, high], axis=dim)
    return block


def shifted(array, axis, by):
    size = lax.axis_size(axis)
    pairs = [(i, i + by) for i in range(size) if 0 <= i + by < size]
    return lax.ppermute(array, axis, pairs)


def tile_from(source_coords, target_coords):
    diff_a = target_coords[0][:, :, None] - source_coords[0][:, None, :]
    diff_b = target_coords[1][:, :, None] - source_coords[1][:, None, :]
    diff_c = target_coords[2][:, :, None] - source_coords[2][:, None, :]
    dist = diff_a * diff_a + diff_b * diff_b + diff_c * diff_c
    return NEAR_GAIN / (BS * jnp.sqrt(dist + SOFT_SQ))


def global_norm(vector):
    return jnp.sqrt(lax.psum(jnp.sum(vector * vector), "patch"))


def finish(beta, basis, columns):
    rotations = []
    target = [beta] + [jnp.float32(0.0) for _ in range(ITERS)]
    upper = []
    for j in range(ITERS):
        column = list(columns[j])
        for i in range(j):
            cos_i, sin_i = rotations[i]
            first = cos_i * column[i] + sin_i * column[i + 1]
            second = -sin_i * column[i] + cos_i * column[i + 1]
            column[i] = first
            column[i + 1] = second
        radius = jnp.sqrt(column[j] * column[j] + column[j + 1] * column[j + 1])
        cos_j = column[j] / radius
        sin_j = column[j + 1] / radius
        column[j] = radius
        rotations.append((cos_j, sin_j))
        target[j + 1] = -sin_j * target[j]
        target[j] = cos_j * target[j]
        upper.append(column[: j + 1])
    coeffs = [jnp.float32(0.0) for _ in range(ITERS)]
    for j in range(ITERS - 1, -1, -1):
        value = target[j]
        for k in range(j + 1, ITERS):
            value = value - upper[k][j] * coeffs[k]
        coeffs[j] = value / upper[j][j]
    solution = coeffs[0] * basis[0]
    j = 1
    solution = solution + coeffs[j] * basis[j]
    return (solution, jnp.abs(target[ITERS]))


def body(
    right_side, coords, diagonal, near_pairs, far_pairs, far_rank, far_left, far_right, far_scale
):
    n_patch = lax.axis_size("patch")
    n_blocks = BLK_DEV * n_patch
    span = BLK_DEV + 2 * RIM
    first = lax.axis_index("patch") * BLK_DEV
    rim_coords = with_halo(coords, (("patch", 1),), RIM * BS)
    coord_blocks = rim_coords.reshape(3, span, BS)
    near_local = near_pairs - first + RIM
    near_groups = near_local.reshape(2, near_pairs.shape[1] // 8, 8).transpose(1, 0, 2)
    far_source = far_pairs[0]
    far_target = far_pairs[1] - first
    rank_columns = jnp.arange(far_scale.shape[1], dtype=jnp.int32)
    weights = far_scale * (rank_columns[None, :] < far_rank[:, None]).astype(jnp.float32)
    left = far_left.astype(jnp.float32)
    right = far_right.astype(jnp.float32)
    span_slots = jnp.arange(span, dtype=jnp.int32)
    hit_target = (far_target[:, None] == jnp.arange(BLK_DEV, dtype=jnp.int32)[None, :]).astype(
        jnp.float32
    )
    hit_source = (far_source[:, None] == jnp.arange(n_blocks, dtype=jnp.int32)[None, :]).astype(
        jnp.float32
    )
    beta = global_norm(right_side)
    basis = [right_side / beta]
    columns = []
    for j in range(ITERS):
        charges = basis[j]
        rim_charges = with_halo(charges, (("patch", 0),), RIM * BS)
        ext_blocks = rim_charges.reshape(span, BS)

        def near_step(total, pairs):
            source = pairs[0]
            target = pairs[1]
            tile = tile_from(coord_blocks[:, source], coord_blocks[:, target])
            to_target = jnp.einsum("pij,pj->pi", tile, ext_blocks[source], precision=HIGH)
            to_source = jnp.einsum("pij,pi->pj", tile, ext_blocks[target], precision=HIGH)
            onto_target = (target[:, None] == span_slots[None, :]).astype(jnp.float32)
            onto_source = (source[:, None] == span_slots[None, :]).astype(jnp.float32)
            total = total + jnp.einsum("pk,pb->kb", onto_target, to_target, precision=HIGH)
            total = total + jnp.einsum("pk,pb->kb", onto_source, to_source, precision=HIGH)
            return (total, None)

        near_total, _ = lax.scan(near_step, jnp.zeros((span, BS), jnp.float32), near_groups)
        whole = lax.all_gather(charges, "patch", axis=0, tiled=True).reshape(n_blocks, BS)
        local = charges.reshape(BLK_DEV, BS)
        coef_t = weights * jnp.einsum("prb,pb->pr", right, whole[far_source], precision=HIGH)
        coef_s = weights * jnp.einsum("prb,pb->pr", left, local[far_target], precision=HIGH)
        to_target = jnp.einsum("prb,pr->pb", left, coef_t, precision=HIGH)
        to_source = jnp.einsum("prb,pr->pb", right, coef_s, precision=HIGH)
        far_own = jnp.einsum("pk,pb->kb", hit_target, to_target, precision=HIGH)
        spread = jnp.einsum("pk,pb->kb", hit_source, to_source, precision=HIGH)
        own_terms = near_total[RIM : RIM + BLK_DEV] + far_own
        from_above = shifted(near_total[:RIM], "patch", -1)
        from_below = shifted(near_total[RIM + BLK_DEV :], "patch", 1)
        own_terms = own_terms.at[BLK_DEV - RIM :].add(from_above)
        own_terms = own_terms.at[:RIM].add(from_below)
        current = lax.dynamic_slice(spread, (first, 0), (BLK_DEV, BS))
        spread = lax.dynamic_update_slice(spread, current + own_terms, (first, 0))
        flat = spread.reshape(n_patch, BLK_DEV * BS)
        mine = lax.psum_scatter(flat, "patch", scatter_dimension=0, tiled=True)
        total = lax.psum(mine, "pair").reshape(-1)
        work = diagonal * charges + total
        heights = []
        for i in range(j + 1):
            height = lax.psum(jnp.sum(basis[i] * work), "patch")
            work = work - height * basis[i]
            heights.append(height)
        below = global_norm(work)
        basis.append(work / below)
        columns.append(heights + [below])
    return finish(beta, basis, columns)


def solution(mesh):
    placed = (
        P("patch"),
        P(None, "patch"),
        P("patch"),
        P(None, ("patch", "pair")),
        P(None, ("patch", "pair")),
        P(("patch", "pair")),
        P(("patch", "pair"), None, None),
        P(("patch", "pair"), None, None),
        P(("patch", "pair"), None),
    )
    return jax.shard_map(
        body, mesh=mesh, in_specs=placed, out_specs=(P("patch"), P()), check_vma=False
    )
```

profile of v0, /device:TPU:1, one launch (start us, length us, event | category | flops | bytes accessed | tf_op | source)
XLA Modules:
  0.0 2093.8 jit_solution(10882445696171735256)
XLA Ops:
  8.6 255.3 %psum.56 = f32[]{:T(128)} all-reduce(f32[]{:T(128)} %multiply_reduce_fusion.5), channel_id=1, replica_groups=mesh['patch'=128,'pair'=4] {'patch'}, use_global_device_ids=true, to_apply=%region_1.0 | all-reduce | flops 1 | bytes 8 | tf_op jit(solution)/shard_map/psum | solution.py:45
  266.7 3.0 collective-permute-start.2
  269.6 5.2 collective-permute-start.3
  275.6 1.9 collective-permute-start
  277.5 2.4 collective-permute-start.1
  284.2 19.6 while.28
  286.1 3.1 fusion.125
  289.7 3.7 fusion.124
  295.9 3.1 fusion.125
  299.5 3.7 fusion.124
  303.8 1.9 collective-permute-start.4
  305.8 3.8 collective-permute-start.5
  309.6 33.6 %all-gather.3.cloned.1.call-done = f32[262144]{0:T(1024)} async-done(((f32[2048]{0:T(1024)}), f32[262144]{0:T(1024)}) %all-gather.3.cloned.1.call-update) | async-done | bytes 1048592 | tf_op jit(solution)/shard_map/all_gather | solution.py:125
  350.3 189.4 %all-reduce.5.cloned.1.call-done = f32[128,2048]{1,0:T(8,128)} async-done(((f32[128,2048]{1,0:T(8,128)}), f32[128,2048]{1,0:T(8,128)}) %all-reduce.5.cloned.1.call-update) | async-done | bytes 1048592
  541.2 8.5 psum.57
  550.3 250.2 %psum.58 = f32[]{:T(128)} all-reduce(f32[]{:T(128)} %multiply_reduce_fusion.4), channel_id=1, replica_groups=mesh['patch'=128,'pair'=4] {'patch'}, use_global_device_ids=true, to_apply=%region_7.8 | all-reduce | flops 1 | bytes 8 | tf_op jit(solution)/shard_map/psum | solution.py:146
  801.7 249.2 %psum.59 = f32[]{:T(128)} all-reduce(f32[]{:T(128)} %get-tuple-element.244), channel_id=1, replica_groups=mesh['patch'=128,'pair'=4] {'patch'}, use_global_device_ids=true, to_apply=%region_9.10 | all-reduce | flops 1 | bytes 8 | tf_op jit(solution)/shard_map/psum | solution.py:45
  1053.0 1.9 collective-permute-start.6
  1054.9 2.4 collective-permute-start.7
  1060.5 19.6 while.29
  1062.4 3.1 fusion.134
  1066.0 3.7 fusion.133
  1072.2 3.1 fusion.134
  1075.8 3.8 fusion.133
  1080.1 1.9 collective-permute-start.8
  1082.1 3.8 collective-permute-start.9
  1085.9 39.2 %all-gather.5.cloned.1.call-done = f32[262144]{0:T(1024)} async-done(((f32[2048]{0:T(1024)}), f32[262144]{0:T(1024)}) %all-gather.5.cloned.1.call-update) | async-done | bytes 1048592 | tf_op jit(solution)/shard_map/all_gather | solution.py:125
  1132.5 189.0 %all-reduce.7.cloned.1.call-done = f32[128,2048]{1,0:T(8,128)} async-done(((f32[128,2048]{1,0:T(8,128)}), f32[128,2048]{1,0:T(8,128)}) %all-reduce.7.cloned.1.call-update) | async-done | bytes 1048592
  1323.0 8.5 psum.60
  1332.2 250.2 %psum.61 = f32[]{:T(128)} all-reduce(f32[]{:T(128)} %multiply_reduce_fusion.2), channel_id=1, replica_groups=mesh['patch'=128,'pair'=4] {'patch'}, use_global_device_ids=true, to_apply=%region_15.16 | all-reduce | flops 1 | bytes 8 | tf_op jit(solution)/shard_map/psum | solution.py:146
  1583.6 249.2 %psum.62 = f32[]{:T(128)} all-reduce(f32[]{:T(128)} %multiply_reduce_fusion.1), channel_id=1, replica_groups=mesh['patch'=128,'pair'=4] {'patch'}, use_global_device_ids=true, to_apply=%region_17.18 | all-reduce | flops 1 | bytes 8 | tf_op jit(solution)/shard_map/psum | solution.py:146
  1837.3 247.3 %psum.63 = f32[]{:T(128)} all-reduce(f32[]{:T(128)} %multiply_reduce_fusion), channel_id=1, replica_groups=mesh['patch'=128,'pair'=4] {'patch'}, use_global_device_ids=true, to_apply=%region_19.20 | all-reduce | flops 1 | bytes 8 | tf_op jit(solution)/shard_map/psum | solution.py:45
  (169 shorter events, 46.1 us)
Async XLA Ops:
  7.2 276.3 %copy-start = (bf16[32,32,256]{2,1,0:T(8,128)(2,1)S(1)}, bf16[32,32,256]{2,1,0:T(8,128)(2,1)}, u32[]{:S(2)}) copy-start(bf16[32,32,256]{2,1,0:T(8,128)(2,1)} %param.27) | copy-start | bytes 1572868
  7.2 277.0 %copy-start.6 = (f32[3,2048]{1,0:T(4,128)S(1)}, f32[3,2048]{1,0:T(4,128)}, u32[]{:S(2)}) copy-start(f32[3,2048]{1,0:T(4,128)} %param.22) | copy-start | bytes 73732
  7.2 336.0 %all-gather.3.cloned.1.call-start = ((), (), s32[]{:S(2)}) async-start(), calls=%async_computation | async-start | bytes 1056768 | tf_op jit(solution)/shard_map/all_gather | solution.py:125
  265.9 18.2 copy-start.4
  265.9 273.8 %all-reduce.5.cloned.1.call-start = ((), (), s32[]{:S(2)}) async-start(), calls=%async_computation.2 | async-start | bytes 2097152
  266.7 17.5 collective-permute-start.2
  269.6 14.5 collective-permute-start.3
  275.6 8.5 collective-permute-start
  277.5 6.6 collective-permute-start.1
  303.8 43.8 %collective-permute-start.4 = (f32[4,256]{1,0:T(4,128)S(1)}, f32[4,256]{1,0:T(4,128)S(1)}, u32[]{:S(2)}, u32[]{:S(2)}) collective-permute-start(f32[4,256]{1,0:T(4,128)S(1)} %get-tuple-element.279), channel_id=1, source_target_pairs={{4,0},{8,4},{12,8},{16,12},{20,16},{24,20},{28,24},{32,28},{36,32}... | collective-permute-start | bytes 12296 | tf_op jit(solution)/shard_map/ppermute | solution.py:33
  305.8 39.6 %copy-start.1 = (bf16[32,32,256]{2,1,0:T(8,128)(2,1)S(1)}, bf16[32,32,256]{2,1,0:T(8,128)(2,1)}, u32[]{:S(2)}) copy-start(bf16[32,32,256]{2,1,0:T(8,128)(2,1)} %param.28) | copy-start | bytes 1572868
  305.8 40.1 %copy-start.7 = (f32[32,32]{1,0:T(8,128)S(1)}, f32[32,32]{1,0:T(8,128)}, u32[]{:S(2)}) copy-start(f32[32,32]{1,0:T(8,128)} %param.29) | copy-start | bytes 12292
  305.8 40.1 %copy-start.8 = (s32[32]{0:T(128)S(1)}, s32[32]{0:T(128)}, u32[]{:S(2)}) copy-start(s32[32]{0:T(128)} %param.26) | copy-start | bytes 388
  305.8 41.8 %collective-permute-start.5 = (f32[4,256]{1,0:T(4,128)S(1)}, f32[4,256]{1,0:T(4,128)S(1)}, u32[]{:S(2)}, u32[]{:S(2)}) collective-permute-start(f32[4,256]{1,0:T(4,128)S(1)} %get-tuple-element.278), channel_id=1, source_target_pairs={{0,4},{4,8},{8,12},{12,16},{16,20},{20,24},{24,28},{28,32},{32,36}... | collective-permute-start | bytes 12296 | tf_op jit(solution)/shard_map/ppermute | solution.py:33
  348.9 200.8 %copy-start.2 = (f32[2048]{0:T(1024)S(1)}, f32[2048]{0:T(1024)}, u32[]{:S(2)}) copy-start(f32[2048]{0:T(1024)} %param.21) | copy-start | bytes 24580
  348.9 200.8 %copy-start.3 = (f32[2048]{0:T(1024)S(1)}, f32[2048]{0:T(1024)}, u32[]{:S(2)}) copy-start(f32[2048]{0:T(1024)} %param.23) | copy-start | bytes 24580
  348.9 776.2 %all-gather.5.cloned.1.call-start = ((), (), s32[]{:S(2)}) async-start(), calls=%async_computation.1 | async-start | bytes 1056768 | tf_op jit(solution)/shard_map/all_gather | solution.py:125
  1051.6 0.6 copy-start.5
  1052.2 269.3 %all-reduce.7.cloned.1.call-start = ((), (), s32[]{:S(2)}) async-start(), calls=%async_computation.3 | async-start | bytes 2097152
  1053.0 5.4 collective-permute-start.6
  1054.9 4.9 collective-permute-start.7
  1080.1 49.3 %collective-permute-start.8 = (f32[4,256]{1,0:T(4,128)S(1)}, f32[4,256]{1,0:T(4,128)S(1)}, u32[]{:S(2)}, u32[]{:S(2)}) collective-permute-start(f32[4,256]{1,0:T(4,128)S(1)} %get-tuple-element.277), channel_id=1, source_target_pairs={{4,0},{8,4},{12,8},{16,12},{20,16},{24,20},{28,24},{32,28},{36,32}... | collective-permute-start | bytes 12296 | tf_op jit(solution)/shard_map/ppermute | solution.py:33
  1082.1 47.4 %collective-permute-start.9 = (f32[4,256]{1,0:T(4,128)S(1)}, f32[4,256]{1,0:T(4,128)S(1)}, u32[]{:S(2)}, u32[]{:S(2)}) collective-permute-start(f32[4,256]{1,0:T(4,128)S(1)} %get-tuple-element.276), channel_id=1, source_target_pairs={{0,4},{4,8},{8,12},{12,16},{16,20},{20,24},{24,28},{28,32},{32,36}... | collective-permute-start | bytes 12296 | tf_op jit(solution)/shard_map/ppermute | solution.py:33
Sparse Core Ops, SparseCore 0:
  266.0 77.1 all-gather.2
  349.0 190.6 all-reduce.4
  1052.3 72.6 all-gather.4
  1130.8 190.6 all-reduce.6
where the time goes:
time: 2100 us; the launch traced here: 2090 us
  blocking collectives  1520 us (72%)
  waiting for transfers between devices  453 us (22%)
  matrix products  34.6 us (2%)
  starting transfers between devices  28.4 us (1%)
  local copies, waits for them, and re-layouts  25.1 us (1%)
  between operations  22 us (1%)
    psum x3, blocking collectives, global_norm(): return jnp.sqrt(lax.psum(jnp.sum(vector * vector), 'patch'))  752 us
    psum x3, blocking collectives, body(): height = lax.psum(jnp.sum(basis[i] * work), 'patch')  750 us
    unnamed x6, waiting for transfers between devices  379 us
    all_gather x2, waiting for transfers between devices, body(): lax.all_gather(charges, 'patch', axis=0, tiled=True).reshape(n_blocks, BS)  72.8 us
  transfers between devices with their start and end apart: 14, of which 5 were waited for; matrix products, arithmetic and copies ran while one was open for 3% of the time, Pallas kernels for 0%

commit v1 on v0

v1 whole, which is shorter than its diff:
```python
import functools

import jax
import jax.numpy as jnp
from jax import lax
from jax.experimental import pallas as pl
from jax.experimental.pallas import tpu as pltpu
from jax.sharding import PartitionSpec as P

BS = 256
BLK_DEV = 8
RIM = 4
RMAX = 32
NEAR_DEV = 16
FAR_DEV = 32
NEAR_GAIN = 2.0
SOFT_SQ = 0.25

N_Y, N_Z, N_X = 8, 8, 4
N_YZ = N_Y * N_Z
ROWS = 4 * N_YZ
SLOTS = BLK_DEV + 2 * RIM
FACT = FAR_DEV * RMAX
KEY = 80

MESH = pl.DeviceIdType.MESH
HIGH = lax.Precision.HIGHEST
F32 = jnp.float32
BF16 = jnp.bfloat16


def place():
    patch = lax.axis_index("patch")
    return lax.axis_index("pair"), patch // (2 * N_Z), (patch // 2) % N_Z, patch % 2


def device(x, y, z, core):
    return {"patch": (y * N_Z + z) * 2 + core, "pair": x}


def send(src, dst, send_sem, recv_sem, to):
    return pltpu.make_async_remote_copy(
        src_ref=src, dst_ref=dst, send_sem=send_sem, recv_sem=recv_sem, device_id=to, device_id_type=MESH
    )


def plane_peer(i, x, y, z, core):
    return device(x, (y + i // N_Z) % N_Y, (z + i % N_Z) % N_Z, core)


def split(value):
    high = value.astype(BF16)
    low = (value - high.astype(F32)).astype(BF16)
    return jnp.concatenate([high, low], axis=0)


def dot(a, b):
    return jnp.dot(a, b, preferred_element_type=F32)


def dot_rows(a, b):
    return lax.dot_general(a, b, (((1,), (1,)), ((), ())), preferred_element_type=F32)


def total(value):
    return jnp.sum(jnp.sum(value, axis=0, keepdims=True), axis=1, keepdims=True)


def kernel(
    near_smem, far_smem, right_ref, coords_ref, diag_ref, near_ref, far_ref, rank_ref, scale_ref,
    left_hbm, right_hbm,
    out_ref, norm_ref,
    left, right, hc, hct, cbc, tiles, hot, weight_d, hit_t,
    gath_a, gath_b, spread_a, spread_b, core_a, core_b, xs_a, xs_b, yz_a, yz_b,
    rows_v, rows_t, rows_y, own, diag, sums_yz, sums_x, sums_c,
    local_sem, halo_sem, gather_sem, scatter_sem, sums_sem,
):
    x, y, z, core = place()
    patch = lax.axis_index("patch")
    n_patch = 2 * N_YZ
    first = patch * BLK_DEV
    yz = y * N_Z + z
    mine = pl.ds(pl.multiple_of(yz * 4, 4), 4)
    up = {"patch": (patch + 1) % n_patch}
    down = {"patch": (patch + n_patch - 1) % n_patch}
    x_peers = [device((x + i) % N_X, y, z, core) for i in range(1, N_X)]
    twin = device(x, y, z, 1 - core)

    barrier = pltpu.get_barrier_semaphore()

    def greet(i, _):
        pl.semaphore_signal(barrier, inc=1, device_id=plane_peer(i, x, y, z, core), device_id_type=MESH)
        return 0

    lax.fori_loop(1, N_YZ, greet, 0)
    for to in x_peers + [twin, up, down]:
        pl.semaphore_signal(barrier, inc=1, device_id=to, device_id_type=MESH)

    load_left = pltpu.make_async_copy(left_hbm, left, local_sem.at[0])
    load_right = pltpu.make_async_copy(right_hbm, right, local_sem.at[1])
    load_left.start()
    load_right.start()

    start = 8 * (x // 2) + x % 2
    for i in range(4):
        gath_a[core, x, pl.ds(yz * 4 + i, 1), :] = right_ref[pl.ds(start + 2 * i, 1), :]
        diag[pl.ds(i, 1), :] = diag_ref[pl.ds(start + 2 * i, 1), :]
    for d in range(3):
        for b in range(BLK_DEV):
            hc[d, RIM + b : RIM + b + 1, :] = coords_ref[d : d + 1, b * BS : (b + 1) * BS]

    pl.semaphore_wait(barrier, N_YZ - 1 + N_X - 1 + 1 + 2)

    halo_up = send(hc.at[:, pl.ds(BLK_DEV, RIM)], hc.at[:, pl.ds(0, RIM)], halo_sem.at[0], halo_sem.at[1], up)
    halo_down = send(
        hc.at[:, pl.ds(RIM, RIM)], hc.at[:, pl.ds(RIM + BLK_DEV, RIM)], halo_sem.at[2], halo_sem.at[3], down
    )
    halo_up.start()
    halo_down.start()

    def wait_rows(ref, sem, n, sent):
        view = ref.at[core, x, pl.ds(0, n)]
        copy = send(view, view, sem, sem, twin)
        if sent:
            copy.wait_send()
        else:
            copy.wait_recv()

    def gather_start(ref, sems):
        own_rows = ref.at[core, x, mine]

        def step(i, _):
            send(own_rows, own_rows, sems.at[0], sems.at[1], plane_peer(i, x, y, z, core)).start()
            return 0

        lax.fori_loop(1, N_YZ, step, 0)

    def gather_middle(ref, sems):
        wait_rows(ref, sems.at[1], ROWS - 4, False)
        for i in range(1, N_X):
            send(ref.at[core, x], ref.at[core, x], sems.at[2], sems.at[2 + i], x_peers[i - 1]).start()

    def gather_end(ref, sems):
        for i in range(1, N_X):
            view = ref.at[core, (x + N_X - i) % N_X]
            send(view, view, sems.at[2], sems.at[2 + i], twin).wait_recv()
        send(ref.at[core], ref.at[core], sems.at[6], sems.at[7], twin).start()
        theirs = ref.at[1 - core]
        copy = send(theirs, theirs, sems.at[6], sems.at[7], twin)
        copy.wait_recv()
        copy.wait_send()
        wait_rows(ref, sems.at[0], ROWS - 4, True)
        for _ in range(1, N_X):
            wait_rows(ref, sems.at[2], ROWS, True)

    gather_start(gath_a, gather_sem.at[0])

    near_f = near_ref[...].astype(F32)
    far_f = far_ref[...].astype(F32)
    lane = lax.broadcasted_iota(jnp.int32, (1, 2 * KEY), 1) % KEY

    def lay(row, count, at):
        pick = lax.broadcasted_iota(jnp.int32, (count, 2 * KEY), 1) % KEY == (
            lax.broadcasted_iota(jnp.int32, (count, 2 * KEY), 0) + at
        )
        return jnp.dot(row, pick.astype(F32), precision=HIGH, preferred_element_type=F32)

    key = lay(near_f, NEAR_DEV, 0)[1:2] + lay(near_f, NEAR_DEV, NEAR_DEV)[0:1]
    key = key + lay(far_f, FAR_DEV, 2 * NEAR_DEV)[0:1]
    key = (key + 0.5).astype(jnp.int32)
    at_own = 2 * NEAR_DEV + FAR_DEV
    key = jnp.where(lane >= at_own, jnp.where(lane < at_own + BLK_DEV, first + lane - at_own, -1), key)
    row = lax.broadcasted_iota(jnp.int32, (ROWS, 2 * KEY), 0)
    for c in range(2):
        for a in range(2):
            block = (row // 4) * 16 + c * 8 + a * 4 + row % 4
            hot[c, a] = (block == key).astype(F32).astype(BF16)

    pair_of = lax.broadcasted_iota(jnp.int32, (FAR_DEV, FACT), 1) // RMAX
    term_of = lax.broadcasted_iota(jnp.int32, (FAR_DEV, FACT), 1) % RMAX
    sub = lax.broadcasted_iota(jnp.int32, (FAR_DEV, FACT), 0)
    eye = lax.broadcasted_iota(jnp.int32, (FAR_DEV, FAR_DEV), 0) == lax.broadcasted_iota(
        jnp.int32, (FAR_DEV, FAR_DEV), 1
    )
    rank_col = jnp.sum(jnp.where(eye, rank_ref[...].astype(F32), 0.0), axis=1, keepdims=True)
    term = lax.broadcasted_iota(jnp.int32, (FAR_DEV, RMAX), 1).astype(F32)
    weights = jnp.where(term < rank_col, scale_ref[...], 0.0)
    spread_w = jnp.dot(weights, (sub == term_of).astype(F32), precision=HIGH, preferred_element_type=F32)
    weight_d[...] = jnp.where(sub == pair_of, spread_w, 0.0)
    target_row = far_ref[1:2, :] - first
    onto = (lax.broadcasted_iota(jnp.int32, (BLK_DEV, FAR_DEV), 0) == target_row).astype(F32)
    hit_t[...] = jnp.dot(onto, (sub == pair_of).astype(F32), preferred_element_type=F32)

    halo_up.wait_recv()
    halo_down.wait_recv()
    for d in range(3):
        hct[pl.ds(SLOTS * d, SLOTS), :] = hc[d]
    turned = hct[...].T
    for b in range(SLOTS):
        for d in range(3):
            at = SLOTS * d + b
            cbc[b, d] = jnp.broadcast_to(turned[:, at : at + 1], (BS, 128))

    def build(k, _):
        source = jnp.clip(near_smem[0, k] - first + RIM, 0, SLOTS - 1)
        target = jnp.clip(near_smem[1, k] - first + RIM, 0, SLOTS - 1)
        for way, (across, along) in enumerate(((source, target), (target, source))):
            line = [hc[d, pl.ds(along, 1), :] for d in range(3)]
            for r in range(0, BS, 64):
                col = [cbc[across, d, r : r + 64, :] for d in range(3)]
                for h in range(2):
                    dist = SOFT_SQ
                    for d in range(3):
                        diff = col[d] - line[d][:, 128 * h : 128 * h + 128]
                        dist = dist + diff * diff
                    tile = (NEAR_GAIN / BS) * lax.rsqrt(dist)
                    high = tile.astype(BF16)
                    tiles[k, way, 0, r : r + 64, 128 * h : 128 * h + 128] = high
                    tiles[k, way, 1, r : r + 64, 128 * h : 128 * h + 128] = (tile - high.astype(F32)).astype(BF16)
        return 0

    lax.fori_loop(0, NEAR_DEV // 2, build, 0)
    gather_middle(gath_a, gather_sem.at[0])
    lax.fori_loop(NEAR_DEV // 2, NEAR_DEV, build, 0)
    gather_end(gath_a, gather_sem.at[0])
    halo_up.wait_send()
    halo_down.wait_send()
    load_left.wait()
    load_right.wait()

    def fetch(ref, s):
        group = s // BLK_DEV
        b = s % BLK_DEV
        at = (group // 2) * 4 + b % 4
        return [ref[group % 2, 2 * (b // 4) + h, pl.ds(at, 1), :] for h in range(2)]

    def product(ref, spread):
        for k in range(NEAR_DEV):
            for h, part in enumerate(fetch(ref, near_smem[0, k])):
                rows_v[k : k + 1, 128 * h : 128 * h + 128] = part
            for h, part in enumerate(fetch(ref, near_smem[1, k])):
                rows_t[k : k + 1, 128 * h : 128 * h + 128] = part
        for k in range(FAR_DEV):
            for h, part in enumerate(fetch(ref, far_smem[0, k])):
                rows_v[NEAR_DEV + k : NEAR_DEV + k + 1, 128 * h : 128 * h + 128] = part
        for a in range(2):
            for h in range(2):
                own[4 * a : 4 * a + 4, 128 * h : 128 * h + 128] = ref[core, 2 * a + h, mine, :]

        far_v = split(rows_v[NEAR_DEV:, :])
        coef = dot_rows(far_v, right[...])
        coef = jnp.sum(weight_d[...] * (coef[:FAR_DEV] + coef[FAR_DEV:]), axis=0, keepdims=True)
        to_own = dot(split(hit_t[...] * coef), left[...])
        rows_y[at_own : at_own + BLK_DEV, :] = to_own[:BLK_DEV] + to_own[BLK_DEV:]
        rows_y[at_own + BLK_DEV :, :] = jnp.zeros((KEY - at_own - BLK_DEV, BS), F32)
        back = dot_rows(split(own[...]), left[...])
        back = jnp.sum(hit_t[...] * (back[:BLK_DEV] + back[BLK_DEV:]), axis=0, keepdims=True)
        to_far = dot(split(weight_d[...] * back), right[...])
        rows_y[2 * NEAR_DEV : at_own, :] = to_far[:FAR_DEV] + to_far[FAR_DEV:]

        near_v = split(rows_v[:NEAR_DEV, :])
        near_t = split(rows_t[...])
        for k in range(NEAR_DEV):
            for way, vectors in enumerate((near_v, near_t)):
                image = dot(vectors, tiles[k, way, 0]) + dot(vectors, tiles[k, way, 1])
                at = way * NEAR_DEV + k
                rows_y[at : at + 1, :] = image[k : k + 1] + image[NEAR_DEV + k : NEAR_DEV + k + 1]

        rows = split(rows_y[...])

        def lay_out(c):
            for a in range(2):
                image = dot(hot[c, a], rows)
                for h in range(2):
                    spread[c, 2 * a + h] = image[:, 128 * h : 128 * h + 128]

        return lay_out

    def scatter(lay_out, spread, core_buf, xs, yzs, sems):
        lay_out(1 - core)
        swap = send(spread.at[1 - core], core_buf, sems.at[0], sems.at[1], twin)
        swap.start()
        lay_out(core)
        swap.wait_recv()
        copies = []
        for i in range(1, N_X):
            q = (x + i) % N_X
            spread[core, q] = spread[core, q] + core_buf[q]
            copy = send(spread.at[core, q], xs.at[i - 1], sems.at[2], sems.at[2 + i], x_peers[i - 1])
            copy.start()
            copies.append(copy)
        spread[core, x] = spread[core, x] + core_buf[x]
        for copy in copies:
            copy.wait_recv()
        spread[core, x] = spread[core, x] + (xs[0] + (xs[1] + xs[2]))
        yzs[mine, :] = spread[core, x, mine, :]

        def step(i, _):
            there = ((y + i // N_Z) % N_Y) * N_Z + (z + i % N_Z) % N_Z
            rows = pl.ds(pl.multiple_of(there * 4, 4), 4)
            send(
                spread.at[core, x, rows], yzs.at[mine], sems.at[6], sems.at[7], plane_peer(i, x, y, z, core)
            ).start()
            return 0

        lax.fori_loop(1, N_YZ, step, 0)
        wait_rows(spread, sems.at[7], ROWS - 4, False)
        wait_rows(spread, sems.at[6], ROWS - 4, True)
        swap.wait_send()
        for copy in copies:
            copy.wait_send()
        image = jnp.sum(yzs[...].reshape(ROWS // 8, 8, 128), axis=0)
        return image[:4] + image[4:]

    def whole_dot(a_ref, b_ref):
        acc = jnp.zeros((8, 128), F32)
        for c in range(2):
            for q in range(4):
                acc = acc + jnp.sum((a_ref[c, q] * b_ref[c, q]).reshape(ROWS // 8, 8, 128), axis=0)
        return total(acc)

    lay_out = product(gath_a, spread_a)
    beta = jnp.sqrt(whole_dot(gath_a, gath_a))
    inv_beta = 1.0 / beta
    image = scatter(lay_out, spread_a, core_a, xs_a, yz_a, scatter_sem.at[0])
    b_mine = gath_a[core, x, mine, :]
    gath_b[core, x, mine, :] = (image + diag[...] * b_mine) * inv_beta

    gather_start(gath_b, gather_sem.at[1])
    gather_middle(gath_b, gather_sem.at[1])
    gather_end(gath_b, gather_sem.at[1])

    h00 = whole_dot(gath_a, gath_b) * inv_beta
    alpha = h00 * inv_beta
    for c in range(2):
        for q in range(4):
            gath_b[c, q] = gath_b[c, q] - alpha * gath_a[c, q]
    h10 = jnp.sqrt(whole_dot(gath_b, gath_b))
    inv_h10 = 1.0 / h10

    lay_out = product(gath_b, spread_b)
    image = scatter(lay_out, spread_b, core_b, xs_b, yz_b, scatter_sem.at[1])
    v0 = b_mine * inv_beta
    w_mine = gath_b[core, x, mine, :]
    v1 = w_mine * inv_h10
    rest = (image + diag[...] * w_mine) * inv_h10 - h10 * v0 - h00 * v1

    def fold(value):
        return jnp.sum(value, axis=0, keepdims=True)

    sums_yz[mine, :] = jnp.concatenate(
        [fold(rest * rest), fold(rest * v0), fold(rest * v1), jnp.zeros((1, 128), F32)], axis=0
    )

    def tell(i, _):
        send(
            sums_yz.at[mine], sums_yz.at[mine], sums_sem.at[0], sums_sem.at[1], plane_peer(i, x, y, z, core)
        ).start()
        return 0

    lax.fori_loop(1, N_YZ, tell, 0)
    most = sums_yz.at[pl.ds(0, ROWS - 4)]
    copy = send(most, most, sums_sem.at[0], sums_sem.at[1], twin)
    copy.wait_recv()
    copy.wait_send()
    acc = jnp.sum(sums_yz[...].reshape(ROWS // 8, 8, 128), axis=0)
    sums_x[x] = acc
    copies = []
    for i in range(1, N_X):
        copy = send(sums_x.at[x], sums_x.at[x], sums_sem.at[2], sums_sem.at[2 + i], x_peers[i - 1])
        copy.start()
        copies.append(copy)
    for i in range(1, N_X):
        view = sums_x.at[(x + N_X - i) % N_X]
        send(view, view, sums_sem.at[2], sums_sem.at[2 + i], twin).wait_recv()
    for copy in copies:
        copy.wait_send()
    sums_c[0] = (sums_x[0] + sums_x[1]) + (sums_x[2] + sums_x[3])
    copy = send(sums_c.at[0], sums_c.at[1], sums_sem.at[6], sums_sem.at[7], twin)
    copy.start()
    copy.wait()
    acc = sums_c[0] + sums_c[1]
    acc = jnp.sum(acc[:4] + acc[4:], axis=1, keepdims=True)
    sq, a0, a1 = acc[0:1], acc[1:2], acc[2:3]
    h01 = h10 + a0
    h11 = h00 + a1
    h21 = jnp.sqrt(jnp.maximum(sq - a0 * a0 - a1 * a1, 0.0))

    rho0 = jnp.sqrt(h00 * h00 + h10 * h10)
    c0 = h00 / rho0
    s0 = h10 / rho0
    r01 = c0 * h01 + s0 * h11
    r11 = c0 * h11 - s0 * h01
    rho1 = jnp.sqrt(r11 * r11 + h21 * h21)
    c1 = r11 / rho1
    s1 = h21 / rho1
    g0 = c0 * beta
    g1 = -s0 * beta
    y1 = c1 * g1 / rho1
    y0 = (g0 - r01 * y1) / rho0
    norm_ref[...] = jnp.broadcast_to(jnp.abs(s1 * g1), (8, 128))
    f0 = y0 * inv_beta
    f1 = y1 * inv_h10
    for a in range(2):
        for h in range(2):
            part = f0 * gath_a[core, 2 * a + h, mine, :] + f1 * gath_b[core, 2 * a + h, mine, :]
            for i in range(4):
                at = 8 * a + 2 * i + h
                out_ref[at : at + 1, :] = part[i : i + 1]


def body(
    right_side, coords, diagonal, near_pairs, far_pairs, far_rank, far_left, far_right, far_scale
):
    vmem = pl.BlockSpec(memory_space=pltpu.VMEM)
    smem = pl.BlockSpec(memory_space=pltpu.SMEM)
    hbm = pl.BlockSpec(memory_space=pl.ANY)
    scratch = [
        pltpu.VMEM((FACT, BS), BF16),
        pltpu.VMEM((FACT, BS), BF16),
        pltpu.VMEM((3, SLOTS, BS), F32),
        pltpu.VMEM((3 * SLOTS, BS), F32),
        pltpu.VMEM((SLOTS, 3, BS, 128), F32),
        pltpu.VMEM((NEAR_DEV, 2, 2, BS, BS), BF16),
        pltpu.VMEM((2, 2, ROWS, 2 * KEY), BF16),
        pltpu.VMEM((FAR_DEV, FACT), F32),
        pltpu.VMEM((BLK_DEV, FACT), F32),
        pltpu.VMEM((2, 4, ROWS, 128), F32),
        pltpu.VMEM((2, 4, ROWS, 128), F32),
        pltpu.VMEM((2, 4, ROWS, 128), F32),
        pltpu.VMEM((2, 4, ROWS, 128), F32),
        pltpu.VMEM((4, ROWS, 128), F32),
        pltpu.VMEM((4, ROWS, 128), F32),
        pltpu.VMEM((3, ROWS, 128), F32),
        pltpu.VMEM((3, ROWS, 128), F32),
        pltpu.VMEM((ROWS, 128), F32),
        pltpu.VMEM((ROWS, 128), F32),
        pltpu.VMEM((NEAR_DEV + FAR_DEV, BS), F32),
        pltpu.VMEM((NEAR_DEV, BS), F32),
        pltpu.VMEM((KEY, BS), F32),
        pltpu.VMEM((BLK_DEV, BS), F32),
        pltpu.VMEM((4, 128), F32),
        pltpu.VMEM((ROWS, 128), F32),
        pltpu.VMEM((4, 8, 128), F32),
        pltpu.VMEM((2, 8, 128), F32),
        pltpu.SemaphoreType.DMA((2,)),
        pltpu.SemaphoreType.DMA((4,)),
        pltpu.SemaphoreType.DMA((2, 8)),
        pltpu.SemaphoreType.DMA((2, 8)),
        pltpu.SemaphoreType.DMA((8,)),
    ]
    solution, norm = pl.pallas_call(
        kernel,
        out_shape=(
            jax.ShapeDtypeStruct((16, 128), F32),
            jax.ShapeDtypeStruct((8, 128), F32),
        ),
        in_specs=[smem, smem, vmem, vmem, vmem, vmem, vmem, vmem, vmem, hbm, hbm],
        out_specs=(vmem, vmem),
        scratch_shapes=scratch,
        compiler_params=pltpu.CompilerParams(
            collective_id=0, has_side_effects=True, vmem_limit_bytes=48 * 1024 * 1024
        ),
        cost_estimate=pl.CostEstimate(flops=100_000_000, bytes_accessed=2_000_000, transcendentals=2_000_000),
        name="gmres",
    )(
        near_pairs, far_pairs, right_side.reshape(16, 128), coords, diagonal.reshape(16, 128), near_pairs,
        far_pairs, far_rank.reshape(1, FAR_DEV), far_scale, far_left.reshape(FACT, BS),
        far_right.reshape(FACT, BS),
    )
    return solution.reshape(BLK_DEV * BS), norm[0, 0]


def solution(mesh):
    placed = (
        P("patch"),
        P(None, "patch"),
        P("patch"),
        P(None, ("patch", "pair")),
        P(None, ("patch", "pair")),
        P(("patch", "pair")),
        P(("patch", "pair"), None, None),
        P(("patch", "pair"), None, None),
        P(("patch", "pair"), None),
    )
    return jax.shard_map(
        body, mesh=mesh, in_specs=placed, out_specs=(P("patch"), P()), check_vma=False
    )
```

time: 2100 us -> 117 us (0.06)
  blocking collectives: 1520 us -> 0 us
  waiting for transfers between devices: 453 us -> 0 us
  Pallas kernels: 0 us -> 108 us
  matrix products: 34.6 us -> 0 us
  starting transfers between devices: 28.4 us -> 0 us
  between operations: 22 us -> 0.67 us
    psum x8 -> x0, blocking collectives: 1520 us -> none  [the longest x3 752 us: global_norm(): return jnp.sqrt(lax.psum(jnp.sum(vector * vector), 'patch'))]
    unnamed x6 -> x0, waiting for transfers between devices: 379 us -> none
    pallas_call x0 -> x1, Pallas kernels: none -> 108 us  [body(): pl.pallas_call(kernel, out_shape=(jax.ShapeDtypeStruct((16, 128), F32), j...]
    all_gather x2 -> x0, waiting for transfers between devices: 72.8 us -> none  [body(): lax.all_gather(charges, 'patch', axis=0, tiled=True).reshape(n_blocks, BS)]
    dot_general x28 -> x0, matrix products: 34.6 us -> none  [the longest x4 15 us: near_step(): jnp.einsum('pij,pj->pi', tile, ext_blocks[source], precision=HIGH)]
    ppermute x10 -> x0, starting transfers between devices: 28.3 us -> none  [the longest x4 11.4 us: shifted(): return lax.ppermute(array, axis, pairs)]
  transfers between devices with their start and end apart: 14 -> 0, of which waited for: 5 -> 0; matrix products, arithmetic and copies ran while one was open for 3% -> 0% of each run, Pallas kernels for 0% -> 0%
where the time goes in v1:
time: 117 us; the launch traced here: 116 us
  Pallas kernels  108 us (92%)
  local copies, waits for them, and re-layouts  7.38 us (6%)
    pallas_call x1, Pallas kernels, body(): pl.pallas_call(kernel, out_shape=(jax.ShapeDtypeStruct((16, 128), F32), j...  108 us
    unnamed x19, local copies, waits for them, and re-layouts  6.87 us

profile of v1, /device:TPU:1, one launch (start us, length us, event | category | flops | bytes accessed | tf_op | source)
XLA Modules:
  0.0 116.5 jit_solution(3899310411334302317)
XLA Ops:
  0.6 0.0 copy-start.4
  0.6 0.0 copy-start.6
  0.7 0.7 copy-done.4
  1.3 0.0 copy-done.6
  1.3 0.0 copy-start
  1.3 1.0 copy-done
  2.4 0.0 copy-start.1
  2.4 1.0 copy-done.1
  3.4 0.0 copy-start.2
  3.4 0.8 copy-done.2
  4.2 0.0 copy-start.3
  4.2 0.7 copy-done.3
  4.9 0.0 copy-start.5
  4.9 0.7 copy-done.5
  5.6 0.0 copy-start.7
  5.6 0.7 copy-done.7
  6.3 0.0 copy-start.8
  6.3 0.7 copy-done.8
  6.9 108.4 %gmres.1 = (f32[16,128]{1,0:T(8,128)S(1)}, f32[8,128]{1,0:T(8,128)S(1)}) custom-call(s32[2,16]{1,0:T(2,128)S(1)} %copy-done.6, s32[2,32]{1,0:T(2,128)S(1)} %copy-done.7, f32[16,128]{1,0:T(8,128)S(1)} %bitcast.10, f32[3,2048]{1,0:T(4,128)S(1)} %copy-done.2, f32[16,128]{1,0:T(8,128)S(1)} %bitcast.11, s32[2,16]{1,0:T(2,128)S(1)} %copy-done.6, ...), custom_call_target="tpu_custom_call" | custom-call | flops 100000000 | bytes 2000000 | tf_op jit(solution)/shard_map/gmres/pallas_call | solution.py:452
  115.4 0.5 slice.3
  115.9 0.6 copy.12
Async XLA Ops:
  0.6 0.7 copy-start.4
  0.6 0.7 copy-start.6
  1.3 1.0 copy-start
  2.4 1.0 copy-start.1
  3.4 0.8 copy-start.2
  4.2 0.7 copy-start.3
  4.9 0.7 copy-start.5
  5.6 0.7 copy-start.7
  6.3 0.7 copy-start.8

commit v2 on v1

v2 whole, which is shorter than its diff:
```python
import functools

import jax
import jax.numpy as jnp
from jax import lax
from jax.experimental import pallas as pl
from jax.experimental.pallas import tpu as pltpu
from jax.sharding import PartitionSpec as P

BS = 256
BLK_DEV = 8
RIM = 4
RMAX = 32
NEAR_DEV = 16
FAR_DEV = 32
NEAR_GAIN = 2.0
SOFT_SQ = 0.25

N_Y, N_Z, N_X = 8, 8, 4
N_YZ = N_Y * N_Z
ROWS = 4 * N_YZ
COLUMN = 2 * N_X
SLOTS = BLK_DEV + 2 * RIM
FACT = FAR_DEV * RMAX
EXTRA = 8

MESH = pl.DeviceIdType.MESH
HIGH = lax.Precision.HIGHEST
F32 = jnp.float32
BF16 = jnp.bfloat16


def place():
    patch = lax.axis_index("patch")
    return lax.axis_index("pair"), patch // (2 * N_Z), (patch // 2) % N_Z, patch % 2


def device(x, y, z, core):
    return {"patch": (y * N_Z + z) * 2 + core, "pair": x}


def send(src, dst, send_sem, recv_sem, to):
    return pltpu.make_async_remote_copy(
        src_ref=src, dst_ref=dst, send_sem=send_sem, recv_sem=recv_sem, device_id=to, device_id_type=MESH
    )


def plane_peer(i, x, y, z, core):
    return device(x, (y + i // N_Z) % N_Y, (z + i % N_Z) % N_Z, core)


def parts(value, count):
    found = []
    for _ in range(count):
        found.append(value.astype(BF16))
        value = value - found[-1].astype(F32)
    return found


def split(value):
    return jnp.concatenate(parts(value, 2), axis=0)


def dot(a, b):
    return jnp.dot(a, b, preferred_element_type=F32)


def dot_rows(a, b):
    return lax.dot_general(a, b, (((1,), (1,)), ((), ())), preferred_element_type=F32)


def fold(value):
    return jnp.sum(value, axis=0, keepdims=True)


def total(value):
    return jnp.sum(fold(value), axis=1, keepdims=True)


def kernel(
    near_smem, right_hbm, coords_hbm, diag_hbm, near_hbm, far_hbm, rank_hbm, scale_hbm, left_hbm, factor_hbm,
    out_ref, norm_ref,
    left, right, right_ref, coords_ref, diag_ref, near_ref, far_ref, rank_ref, scale_ref,
    hc, hct, cbc, tiles, keys, hot, hot_t, weight_d, hit_t,
    quarter, picked, got, given, taken, spread, landed, span, rim, joined,
    rows_n, sums_yz, sums_c,
    local_sem, once_sem, step_sem, sums_sem,
):
    x, y, z, core = place()
    patch = lax.axis_index("patch")
    n_patch = 2 * N_YZ
    first = patch * BLK_DEV
    yz = y * N_Z + z
    me = 2 * x + core
    mine = pl.ds(pl.multiple_of(yz * 4, 4), 4)
    up = {"patch": (patch + 1) % n_patch}
    down = {"patch": (patch + n_patch - 1) % n_patch}
    x_peers = [device((x + i) % N_X, y, z, core) for i in range(1, N_X)]
    twin = device(x, y, z, 1 - core)
    column = []
    for i in range(1, COLUMN):
        other_x, other_core = (x + i // 2) % N_X, (core + i) % 2
        column.append((2 * other_x + other_core, other_x % 2, device(other_x, y, z, other_core)))

    barrier = pltpu.get_barrier_semaphore()

    def greet(i, _):
        pl.semaphore_signal(barrier, inc=1, device_id=plane_peer(i, x, y, z, core), device_id_type=MESH)
        return 0

    loads = [
        pltpu.make_async_copy(src, dst, local_sem.at[i])
        for i, (src, dst) in enumerate(
            (
                (left_hbm, left), (factor_hbm, right), (right_hbm, right_ref), (coords_hbm, coords_ref),
                (diag_hbm, diag_ref), (near_hbm, near_ref), (far_hbm, far_ref), (rank_hbm, rank_ref),
                (scale_hbm, scale_ref),
            )
        )
    ]
    for load in loads:
        load.start()
    lax.fori_loop(1, N_YZ, greet, 0)
    for _, _, to in column:
        pl.semaphore_signal(barrier, inc=1, device_id=to, device_id_type=MESH)
    for to in (up, down):
        pl.semaphore_signal(barrier, inc=1, device_id=to, device_id_type=MESH)
    for load in loads:
        load.wait()

    def natural(ref):
        return jnp.concatenate([ref[pl.ds(h, BLK_DEV, stride=2), :] for h in range(2)], axis=1)

    def own_quarter(value):
        found = value[:4, :128]
        for q in range(1, N_X):
            a, h = q // 2, q % 2
            found = jnp.where(x == q, value[4 * a : 4 * a + 4, 128 * h : 128 * h + 128], found)
        return found

    b_own = natural(right_ref)
    diag = natural(diag_ref)
    span[0, RIM : RIM + BLK_DEV, :] = b_own
    quarter[0, mine, :] = own_quarter(b_own)
    for d in range(3):
        for b in range(BLK_DEV):
            hc[d, RIM + b : RIM + b + 1, :] = coords_ref[d : d + 1, b * BS : (b + 1) * BS]

    near_f = near_ref[...].astype(F32)
    far_f = far_ref[...].astype(F32)
    sub_key = lax.broadcasted_iota(jnp.int32, (FAR_DEV, COLUMN * FAR_DEV), 0)
    lane_key = lax.broadcasted_iota(jnp.int32, (FAR_DEV, COLUMN * FAR_DEV), 1)
    pick = (lane_key == sub_key + me * FAR_DEV).astype(F32)
    laid = jnp.dot(far_f, pick, precision=HIGH, preferred_element_type=F32)
    keys[me] = jnp.broadcast_to(laid[0:1], (8, COLUMN * FAR_DEV))

    pair_of = lax.broadcasted_iota(jnp.int32, (FAR_DEV, FACT), 1) // RMAX
    term_of = lax.broadcasted_iota(jnp.int32, (FAR_DEV, FACT), 1) % RMAX
    sub = lax.broadcasted_iota(jnp.int32, (FAR_DEV, FACT), 0)
    eye = lax.broadcasted_iota(jnp.int32, (FAR_DEV, FAR_DEV), 0) == lax.broadcasted_iota(
        jnp.int32, (FAR_DEV, FAR_DEV), 1
    )
    rank_col = jnp.sum(jnp.where(eye, rank_ref[...].astype(F32), 0.0), axis=1, keepdims=True)
    term = lax.broadcasted_iota(jnp.int32, (FAR_DEV, RMAX), 1).astype(F32)
    weights = jnp.where(term < rank_col, scale_ref[...], 0.0)
    spread_w = jnp.dot(weights, (sub == term_of).astype(F32), precision=HIGH, preferred_element_type=F32)
    weight_d[...] = jnp.where(sub == pair_of, spread_w, 0.0)
    target_row = far_ref[1:2, :] - first
    onto = (lax.broadcasted_iota(jnp.int32, (BLK_DEV, FAR_DEV), 0) == target_row).astype(F32)
    hit_t[...] = jnp.dot(onto, (sub == pair_of).astype(F32), preferred_element_type=F32)

    def wait_for(view, sem, sent):
        copy = send(view, view, sem, sem, twin)
        if sent:
            copy.wait_send()
        else:
            copy.wait_recv()

    def plane(step, sems):
        def each(i, _):
            src, dst = step(((y + i // N_Z) % N_Y) * N_Z + (z + i % N_Z) % N_Z)
            send(src, dst, sems[0], sems[1], plane_peer(i, x, y, z, core)).start()
            return 0

        lax.fori_loop(1, N_YZ, each, 0)

    def give(it, own_value):
        back = dot_rows(split(own_value), left[...])
        back = fold(hit_t[...] * (back[:BLK_DEV] + back[BLK_DEV:]))
        to_far = dot(split(weight_d[...] * back), right[...])
        to_far = to_far[:FAR_DEV] + to_far[FAR_DEV:]
        for h in range(2):
            given[it, h] = to_far[:, 128 * h : 128 * h + 128]
        taken[it, me] = given[it, x % 2]

    def give_start(it):
        for number, half, to in column:
            send(given.at[it, half], taken.at[it, me], step_sem.at[it, 0], step_sem.at[it, 1], to).start()

    def gather_start(it):
        own_rows = quarter.at[it, mine]
        plane(lambda there: (own_rows, own_rows), (step_sem.at[it, 2], step_sem.at[it, 3]))

    def span_start(it):
        send(
            span.at[it, pl.ds(BLK_DEV, RIM)], span.at[it, pl.ds(0, RIM)],
            step_sem.at[it, 4], step_sem.at[it, 5], up,
        ).start()
        send(
            span.at[it, pl.ds(RIM, RIM)], span.at[it, pl.ds(RIM + BLK_DEV, RIM)],
            step_sem.at[it, 6], step_sem.at[it, 7], down,
        ).start()

    def scatter_plane(it):
        wait_for(taken.at[it, pl.ds(0, COLUMN - 1)], step_sem.at[it, 1], False)
        value = 0.0
        for part in parts(taken[it].reshape(COLUMN * FAR_DEV, 128), 3):
            value = value + dot(hot[...], part)
        spread[it] = value
        landed[it, mine, :] = spread[it, mine, :]
        plane(
            lambda there: (spread.at[it, pl.ds(pl.multiple_of(there * 4, 4), 4)], landed.at[it, mine]),
            (step_sem.at[it, 8], step_sem.at[it, 9]),
        )

    def gather_column(it, extras):
        wait_for(quarter.at[it, pl.ds(0, ROWS - 4)], step_sem.at[it, 3], False)
        value = 0.0
        for part in parts(quarter[it], 3):
            value = value + dot(hot_t[...], part)
        picked[it, :, pl.ds(0, FAR_DEV), :] = value.reshape(COLUMN, FAR_DEV, 128)
        sums = [fold(quarter[i] * quarter[j]) for i, j in extras]
        sums = jnp.concatenate(sums + [jnp.zeros((EXTRA - len(sums), 128), F32)], axis=0)
        for g in range(COLUMN):
            picked[it, g, pl.ds(FAR_DEV, EXTRA), :] = sums
        got[it, me] = picked[it, me]
        for number, half, to in column:
            send(picked.at[it, number], got.at[it, me], step_sem.at[it, 10], step_sem.at[it, 11], to).start()

    def gather_end(it):
        wait_for(got.at[it, pl.ds(0, COLUMN - 1)], step_sem.at[it, 11], False)
        halves = []
        for h in range(2):
            at = 2 * h
            halves.append((got[it, at] + got[it, at + 1]) + (got[it, at + 4] + got[it, at + 5]))
        sums = jnp.sum(halves[0][FAR_DEV:] + halves[1][FAR_DEV:], axis=1, keepdims=True)
        far_v = split(jnp.concatenate([half[:FAR_DEV] for half in halves], axis=1))
        coef = dot_rows(far_v, right[...])
        coef = fold(weight_d[...] * (coef[:FAR_DEV] + coef[FAR_DEV:]))
        to_own = dot(split(hit_t[...] * coef), left[...])
        return to_own[:BLK_DEV] + to_own[BLK_DEV:], sums

    def near(it):
        wait_for(span.at[it, pl.ds(0, RIM)], step_sem.at[it, 5], False)
        wait_for(span.at[it, pl.ds(0, RIM)], step_sem.at[it, 7], False)
        vectors = []
        for way in range(2):
            rows = [
                span[it, pl.ds(jnp.clip(near_smem[way, k] - first + RIM, 0, SLOTS - 1), 1), :]
                for k in range(NEAR_DEV)
            ]
            vectors.append(split(jnp.concatenate(rows, axis=0)))
        for k in range(NEAR_DEV):
            for way in range(2):
                image = dot(vectors[way], tiles[k, way, 0]) + dot(vectors[way], tiles[k, way, 1])
                at = way * NEAR_DEV + k
                rows_n[at : at + 1, :] = image[k : k + 1] + image[NEAR_DEV + k : NEAR_DEV + k + 1]
        slot = lax.broadcasted_iota(jnp.int32, (SLOTS, NEAR_DEV), 0)
        hits = [(slot == near_ref[way : way + 1, :] - first + RIM).astype(F32) for way in (1, 0)]
        hits = jnp.concatenate(hits, axis=1).astype(BF16)
        value = 0.0
        for part in parts(rows_n[...], 3):
            value = value + dot(hits, part)
        rim[it, 0] = value
        send(
            rim.at[it, 0, pl.ds(0, RIM)], rim.at[it, 1, pl.ds(RIM, RIM)],
            step_sem.at[it, 12], step_sem.at[it, 13], down,
        ).start()
        send(
            rim.at[it, 0, pl.ds(RIM + BLK_DEV, RIM)], rim.at[it, 1, pl.ds(0, RIM)],
            step_sem.at[it, 14], step_sem.at[it, 15], up,
        ).start()

    def join(it, far_own):
        wait_for(rim.at[it, 1, pl.ds(0, RIM)], step_sem.at[it, 13], False)
        wait_for(rim.at[it, 1, pl.ds(0, RIM)], step_sem.at[it, 15], False)
        local = far_own + rim[it, 0, RIM : RIM + BLK_DEV, :] + rim[it, 1, 0:BLK_DEV, :]
        wait_for(landed.at[it, pl.ds(0, ROWS - 4)], step_sem.at[it, 9], False)
        image = jnp.sum(landed[it].reshape(ROWS // 8, 8, 128), axis=0)
        image = image[:4] + image[4:]
        image = jnp.concatenate([image, image], axis=0)
        image = jnp.concatenate([image, image], axis=1)
        at_row = lax.broadcasted_iota(jnp.int32, (BLK_DEV, BS), 0) // 4
        at_half = lax.broadcasted_iota(jnp.int32, (BLK_DEV, BS), 1) // 128
        joined[it, x] = local + jnp.where(2 * at_row + at_half == x, image, 0.0)
        for i in (2, 1, 3):
            send(
                joined.at[it, x], joined.at[it, x], step_sem.at[it, 16], step_sem.at[it, 16 + i], x_peers[i - 1]
            ).start()
        for i in range(1, N_X):
            wait_for(joined.at[it, (x + N_X - i) % N_X], step_sem.at[it, 16 + i], False)
        return (joined[it, 0] + joined[it, 1]) + (joined[it, 2] + joined[it, 3])

    def sent(it):
        wait_for(taken.at[it, pl.ds(0, COLUMN - 1)], step_sem.at[it, 0], True)
        wait_for(quarter.at[it, pl.ds(0, ROWS - 4)], step_sem.at[it, 2], True)
        wait_for(span.at[it, pl.ds(0, RIM)], step_sem.at[it, 4], True)
        wait_for(span.at[it, pl.ds(0, RIM)], step_sem.at[it, 6], True)
        wait_for(landed.at[it, pl.ds(0, ROWS - 4)], step_sem.at[it, 8], True)
        wait_for(got.at[it, pl.ds(0, COLUMN - 1)], step_sem.at[it, 10], True)
        wait_for(rim.at[it, 1, pl.ds(0, RIM)], step_sem.at[it, 12], True)
        wait_for(rim.at[it, 1, pl.ds(0, RIM)], step_sem.at[it, 14], True)
        wait_for(joined.at[it, pl.ds(0, N_X - 1)], step_sem.at[it, 16], True)

    def build(k, _):
        source = jnp.clip(near_smem[0, k] - first + RIM, 0, SLOTS - 1)
        target = jnp.clip(near_smem[1, k] - first + RIM, 0, SLOTS - 1)
        for way, (across, along) in enumerate(((source, target), (target, source))):
            line = [hc[d, pl.ds(along, 1), :] for d in range(3)]
            for r in range(0, BS, 64):
                col = [cbc[across, d, r : r + 64, :] for d in range(3)]
                for h in range(2):
                    dist = SOFT_SQ
                    for d in range(3):
                        diff = col[d] - line[d][:, 128 * h : 128 * h + 128]
                        dist = dist + diff * diff
                    tile = (NEAR_GAIN / BS) * lax.rsqrt(dist)
                    high = tile.astype(BF16)
                    tiles[k, way, 0, r : r + 64, 128 * h : 128 * h + 128] = high
                    tiles[k, way, 1, r : r + 64, 128 * h : 128 * h + 128] = (tile - high.astype(F32)).astype(BF16)
        return 0

    give(0, b_own)
    pl.semaphore_wait(barrier, N_YZ - 1 + COLUMN - 1 + 2)

    for number, half, to in column:
        send(keys.at[me], keys.at[me], once_sem.at[0], once_sem.at[1], to).start()
    give_start(0)
    halo_up = send(hc.at[:, pl.ds(BLK_DEV, RIM)], hc.at[:, pl.ds(0, RIM)], once_sem.at[2], once_sem.at[3], up)
    halo_down = send(
        hc.at[:, pl.ds(RIM, RIM)], hc.at[:, pl.ds(RIM + BLK_DEV, RIM)], once_sem.at[4], once_sem.at[5], down
    )
    halo_up.start()
    halo_down.start()
    gather_start(0)
    span_start(0)
    wait_for(keys.at[pl.ds(0, COLUMN - 1)], once_sem.at[1], False)
    key = keys[0]
    for g in range(1, COLUMN):
        key = key + keys[g]
    key = (key[0:1] + 0.5).astype(jnp.int32)
    row = lax.broadcasted_iota(jnp.int32, (ROWS, COLUMN * FAR_DEV), 0)
    block = (row // 4) * 16 + core * 8 + (x // 2) * 4 + row % 4
    hits = (block == key).astype(F32)
    hot[...] = hits.astype(BF16)
    hot_t[...] = hits.T.astype(BF16)
    scatter_plane(0)

    halo_up.wait_recv()
    halo_down.wait_recv()
    for d in range(3):
        hct[pl.ds(SLOTS * d, SLOTS), :] = hc[d]
    turned = hct[...].T
    for b in range(SLOTS):
        for d in range(3):
            at = SLOTS * d + b
            cbc[b, d] = jnp.broadcast_to(turned[:, at : at + 1], (BS, 128))
    lax.fori_loop(0, NEAR_DEV // 4, build, 0)
    gather_column(0, ((0, 0),))
    lax.fori_loop(NEAR_DEV // 4, NEAR_DEV, build, 0)
    near(0)
    far_own, sums = gather_end(0)
    beta = jnp.sqrt(sums[0:1])
    inv_beta = 1.0 / beta
    w_own = (join(0, far_own) + diag * b_own) * inv_beta

    span[1, RIM : RIM + BLK_DEV, :] = w_own
    quarter[1, mine, :] = own_quarter(w_own)
    give(1, w_own)
    give_start(1)
    span_start(1)
    gather_start(1)
    wait_for(keys.at[pl.ds(0, COLUMN - 1)], once_sem.at[0], True)
    halo_up.wait_send()
    halo_down.wait_send()
    sent(0)
    scatter_plane(1)
    near(1)
    gather_column(1, ((0, 1), (1, 1)))
    far_own, sums = gather_end(1)
    h00 = sums[0:1] * inv_beta
    shift = sums[1:2] - h00 * h00
    v0 = b_own * inv_beta
    u = w_own - h00 * v0
    rest = join(1, far_own) + diag * w_own - h00 * w_own - shift * v0 - h00 * u

    def lanes(value):
        value = fold(value)
        return value[:, :128] + value[:, 128:]

    sums_yz[mine, :] = jnp.concatenate(
        [lanes(rest * rest), lanes(rest * v0), lanes(rest * u), lanes(u * u)], axis=0
    )
    own_sums = sums_yz.at[mine]
    plane(lambda there: (own_sums, own_sums), (sums_sem.at[0], sums_sem.at[1]))
    sent(1)
    wait_for(sums_yz.at[pl.ds(0, ROWS - 4)], sums_sem.at[1], False)
    wait_for(sums_yz.at[pl.ds(0, ROWS - 4)], sums_sem.at[0], True)
    sums_c[0] = jnp.sum(sums_yz[...].reshape(ROWS // 8, 8, 128), axis=0)
    copy = send(sums_c.at[0], sums_c.at[1], sums_sem.at[2], sums_sem.at[3], twin)
    copy.start()
    copy.wait()
    acc = sums_c[0] + sums_c[1]
    acc = jnp.sum(acc[:4] + acc[4:], axis=1, keepdims=True)
    sq, a0, a1, uu = acc[0:1], acc[1:2], acc[2:3], acc[3:4]
    h10 = jnp.sqrt(uu)
    inv_h10 = 1.0 / h10
    a1 = a1 * inv_h10
    h01 = (shift + a0) * inv_h10
    h11 = h00 + a1 * inv_h10
    h21 = jnp.sqrt(jnp.maximum(sq - a0 * a0 - a1 * a1, 0.0)) * inv_h10

    rho0 = jnp.sqrt(h00 * h00 + h10 * h10)
    c0 = h00 / rho0
    s0 = h10 / rho0
    r01 = c0 * h01 + s0 * h11
    r11 = c0 * h11 - s0 * h01
    rho1 = jnp.sqrt(r11 * r11 + h21 * h21)
    c1 = r11 / rho1
    s1 = h21 / rho1
    g0 = c0 * beta
    g1 = -s0 * beta
    y1 = c1 * g1 / rho1
    y0 = (g0 - r01 * y1) / rho0
    norm_ref[...] = jnp.abs(s1 * g1)
    answer = y0 * v0 + (y1 * inv_h10) * u
    for h in range(2):
        out_ref[pl.ds(h, BLK_DEV, stride=2), :] = answer[:, 128 * h : 128 * h + 128]


def body(
    right_side, coords, diagonal, near_pairs, far_pairs, far_rank, far_left, far_right, far_scale
):
    vmem = pl.BlockSpec(memory_space=pltpu.VMEM)
    smem = pl.BlockSpec(memory_space=pltpu.SMEM)
    hbm = pl.BlockSpec(memory_space=pltpu.HBM)
    width = COLUMN * FAR_DEV
    scratch = [
        pltpu.VMEM((FACT, BS), BF16),
        pltpu.VMEM((FACT, BS), BF16),
        pltpu.VMEM((16, 128), F32),
        pltpu.VMEM((3, BLK_DEV * BS), F32),
        pltpu.VMEM((16, 128), F32),
        pltpu.VMEM((2, NEAR_DEV), jnp.int32),
        pltpu.VMEM((2, FAR_DEV), jnp.int32),
        pltpu.VMEM((1, FAR_DEV), jnp.int32),
        pltpu.VMEM((FAR_DEV, RMAX), F32),
        pltpu.VMEM((3, SLOTS, BS), F32),
        pltpu.VMEM((3 * SLOTS, BS), F32),
        pltpu.VMEM((SLOTS, 3, BS, 128), F32),
        pltpu.VMEM((NEAR_DEV, 2, 2, BS, BS), BF16),
        pltpu.VMEM((COLUMN, 8, width), F32),
        pltpu.VMEM((ROWS, width), BF16),
        pltpu.VMEM((width, ROWS), BF16),
        pltpu.VMEM((FAR_DEV, FACT), F32),
        pltpu.VMEM((BLK_DEV, FACT), F32),
        pltpu.VMEM((2, ROWS, 128), F32),
        pltpu.VMEM((2, COLUMN, FAR_DEV + EXTRA, 128), F32),
        pltpu.VMEM((2, COLUMN, FAR_DEV + EXTRA, 128), F32),
        pltpu.VMEM((2, 2, FAR_DEV, 128), F32),
        pltpu.VMEM((2, COLUMN, FAR_DEV, 128), F32),
        pltpu.VMEM((2, ROWS, 128), F32),
        pltpu.VMEM((2, ROWS, 128), F32),
        pltpu.VMEM((2, SLOTS, BS), F32),
        pltpu.VMEM((2, 2, SLOTS, BS), F32),
        pltpu.VMEM((2, N_X, BLK_DEV, BS), F32),
        pltpu.VMEM((2 * NEAR_DEV, BS), F32),
        pltpu.VMEM((ROWS, 128), F32),
        pltpu.VMEM((2, 8, 128), F32),
        pltpu.SemaphoreType.DMA((9,)),
        pltpu.SemaphoreType.DMA((6,)),
        pltpu.SemaphoreType.DMA((2, 20)),
        pltpu.SemaphoreType.DMA((4,)),
    ]
    solution, norm = pl.pallas_call(
        kernel,
        out_shape=(
            jax.ShapeDtypeStruct((16, 128), F32),
            jax.ShapeDtypeStruct((1, 1), F32),
        ),
        in_specs=[smem] + [hbm] * 9,
        out_specs=(vmem, vmem),
        scratch_shapes=scratch,
        compiler_params=pltpu.CompilerParams(
            collective_id=0, has_side_effects=True, vmem_limit_bytes=60 * 1024 * 1024
        ),
        cost_estimate=pl.CostEstimate(flops=100_000_000, bytes_accessed=2_000_000, transcendentals=2_000_000),
        name="gmres",
    )(
        near_pairs, right_side.reshape(16, 128), coords, diagonal.reshape(16, 128), near_pairs,
        far_pairs, far_rank.reshape(1, FAR_DEV), far_scale, far_left.reshape(FACT, BS),
        far_right.reshape(FACT, BS),
    )
    return solution.reshape(BLK_DEV * BS), norm.reshape(())


def solution(mesh):
    placed = (
        P("patch"),
        P(None, "patch"),
        P("patch"),
        P(None, ("patch", "pair")),
        P(None, ("patch", "pair")),
        P(("patch", "pair")),
        P(("patch", "pair"), None, None),
        P(("patch", "pair"), None, None),
        P(("patch", "pair"), None),
    )
    return jax.shard_map(
        body, mesh=mesh, in_specs=placed, out_specs=(P("patch"), P()), check_vma=False
    )
```

time: 117 us -> 72.6 us (0.62)
  Pallas kernels: 108 us -> 68.7 us
  local copies, waits for them, and re-layouts: 7.38 us -> 1.3 us
  between operations: 0.67 us -> 2.41 us
    pallas_call x1, Pallas kernels: 108 us -> 68.7 us  [body(): pl.pallas_call(kernel, out_shape=(jax.ShapeDtypeStruct((16, 128), F32), j...]
    unnamed x19 -> x1, local copies, waits for them, and re-layouts: 6.87 us -> 1.3 us
where the time goes in v2:
time: 72.6 us; the launch traced here: 72.4 us
  Pallas kernels  68.7 us (95%)
  between operations  2.41 us (3%)
  local copies, waits for them, and re-layouts  1.3 us (2%)
    pallas_call x1, Pallas kernels, body(): pl.pallas_call(kernel, out_shape=(jax.ShapeDtypeStruct((16, 128), F32), j...  68.7 us

profile of v2, /device:TPU:1, one launch (start us, length us, event | category | flops | bytes accessed | tf_op | source)
XLA Modules:
  0.0 72.4 jit_solution(8901749110385586579)
XLA Ops:
  0.6 68.7 %gmres.1 = (f32[16,128]{1,0:T(8,128)}, f32[1,1]{1,0:T(1,128)}) custom-call(s32[2,16]{1,0:T(2,128)} %near_hbm.1, f32[16,128]{1,0:T(8,128)} %bitcast.10, f32[3,2048]{1,0:T(4,128)} %coords_hbm.1, f32[16,128]{1,0:T(8,128)} %bitcast.11, s32[2,16]{1,0:T(2,128)} %near_hbm.1, s32[2,32]{1,0:T(2,128)} %far_hbm.1, s32[1,32]{1,0:T(1,128)} %bitcast.12, ...), custom_call_target="tpu_custom_call" | custom-call | flops 100000000 | bytes 2000000 | tf_op jit(solution)/shard_map/gmres/pallas_call | solution.py:485
  69.3 1.3 %copy.13 = f32[2048]{0:T(1024)} copy(f32[2048]{0:T(1024)} %bitcast.7) | data formatting | bytes 16384

commit v3 on v2

--- a/solution.py
+++ b/solution.py
@@ -45,8 +45,8 @@
     )
 
 
-def plane_peer(i, x, y, z, core):
-    return device(x, (y + i // N_Z) % N_Y, (z + i % N_Z) % N_Z, core)
+def far_first(n):
+    return sorted(range(n), key=lambda d: -min(d, n - d))
 
 
 def parts(value, count):
@@ -98,16 +98,36 @@
     x_peers = [device((x + i) % N_X, y, z, core) for i in range(1, N_X)]
     twin = device(x, y, z, 1 - core)
     column = []
-    for i in range(1, COLUMN):
+    for i in (4, 5, 2, 3, 6, 7, 1):
         other_x, other_core = (x + i // 2) % N_X, (core + i) % 2
         column.append((2 * other_x + other_core, other_x % 2, device(other_x, y, z, other_core)))
 
     barrier = pltpu.get_barrier_semaphore()
 
-    def greet(i, _):
-        pl.semaphore_signal(barrier, inc=1, device_id=plane_peer(i, x, y, z, core), device_id_type=MESH)
-        return 0
-
+    z_peers = [((z + d) % N_Z, d) for d in far_first(N_Z)]
+
+    def over_plane(act):
+        def rows(k, _):
+            other_y = (y + N_Y // 2 + ((k + 1) // 2) * (1 - 2 * (k % 2))) % N_Y
+            for other_z, _ in z_peers:
+                act(other_y, other_z)
+            return 0
+
+        lax.fori_loop(0, N_Y - 1, rows, 0)
+        for other_z, d in z_peers:
+            if d:
+                act(y, other_z)
+
+    def greet(other_y, other_z):
+        pl.semaphore_signal(
+            barrier, inc=1, device_id=device(x, other_y, other_z, core), device_id_type=MESH
+        )
+
+    over_plane(greet)
+    for _, _, to in column:
+        pl.semaphore_signal(barrier, inc=1, device_id=to, device_id_type=MESH)
+    for to in (up, down):
+        pl.semaphore_signal(barrier, inc=1, device_id=to, device_id_type=MESH)
     loads = [
         pltpu.make_async_copy(src, dst, local_sem.at[i])
         for i, (src, dst) in enumerate(
@@ -120,11 +140,6 @@
     ]
     for load in loads:
         load.start()
-    lax.fori_loop(1, N_YZ, greet, 0)
-    for _, _, to in column:
-        pl.semaphore_signal(barrier, inc=1, device_id=to, device_id_type=MESH)
-    for to in (up, down):
-        pl.semaphore_signal(barrier, inc=1, device_id=to, device_id_type=MESH)
     for load in loads:
         load.wait()
 
@@ -177,12 +192,11 @@
             copy.wait_recv()
 
     def plane(step, sems):
-        def each(i, _):
-            src, dst = step(((y + i // N_Z) % N_Y) * N_Z + (z + i % N_Z) % N_Z)
-            send(src, dst, sems[0], sems[1], plane_peer(i, x, y, z, core)).start()
-            return 0
-
-        lax.fori_loop(1, N_YZ, each, 0)
+        def each(other_y, other_z):
+            src, dst = step(other_y * N_Z + other_z)
+            send(src, dst, sems[0], sems[1], device(x, other_y, other_z, core)).start()
+
+        over_plane(each)
 
     def give(it, own_value):
         back = dot_rows(split(own_value), left[...])

time: 72.6 us -> 66.9 us (0.921)
  Pallas kernels: 68.7 us -> 63 us
    pallas_call x1, Pallas kernels: 68.7 us -> 63 us  [body(): pl.pallas_call(kernel, out_shape=(jax.ShapeDtypeStruct((16, 128), F32), j...]
where the time goes in v3:
time: 66.9 us; the launch traced here: 66.7 us
  Pallas kernels  63 us (94%)
  between operations  2.41 us (4%)
  local copies, waits for them, and re-layouts  1.3 us (2%)
    pallas_call x1, Pallas kernels, body(): pl.pallas_call(kernel, out_shape=(jax.ShapeDtypeStruct((16, 128), F32), j...  63 us

profile of v3, /device:TPU:1, one launch (start us, length us, event | category | flops | bytes accessed | tf_op | source)
XLA Modules:
  0.0 66.7 jit_solution(1492896037041869196)
XLA Ops:
  0.6 63.0 %gmres.1 = (f32[16,128]{1,0:T(8,128)}, f32[1,1]{1,0:T(1,128)}) custom-call(s32[2,16]{1,0:T(2,128)} %near_hbm.1, f32[16,128]{1,0:T(8,128)} %bitcast.10, f32[3,2048]{1,0:T(4,128)} %coords_hbm.1, f32[16,128]{1,0:T(8,128)} %bitcast.11, s32[2,16]{1,0:T(2,128)} %near_hbm.1, s32[2,32]{1,0:T(2,128)} %far_hbm.1, s32[1,32]{1,0:T(1,128)} %bitcast.12, ...), custom_call_target="tpu_custom_call" | custom-call | flops 100000000 | bytes 2000000 | tf_op jit(solution)/shard_map/gmres/pallas_call | solution.py:499
  63.6 1.3 %copy.13 = f32[2048]{0:T(1024)} copy(f32[2048]{0:T(1024)} %bitcast.7) | data formatting | bytes 16384

commit v4 on v3

--- a/solution.py
+++ b/solution.py
@@ -275,8 +275,8 @@
             ]
             vectors.append(split(jnp.concatenate(rows, axis=0)))
         for k in range(NEAR_DEV):
-            for way in range(2):
-                image = dot(vectors[way], tiles[k, way, 0]) + dot(vectors[way], tiles[k, way, 1])
+            for way, multiply in enumerate((dot_rows, dot)):
+                image = multiply(vectors[way], tiles[k, 0]) + multiply(vectors[way], tiles[k, 1])
                 at = way * NEAR_DEV + k
                 rows_n[at : at + 1, :] = image[k : k + 1] + image[NEAR_DEV + k : NEAR_DEV + k + 1]
         slot = lax.broadcasted_iota(jnp.int32, (SLOTS, NEAR_DEV), 0)
@@ -328,23 +328,29 @@
 
     def build(k, _):
         source = jnp.clip(near_smem[0, k] - first + RIM, 0, SLOTS - 1)
-        target = jnp.clip(near_smem[1, k] - first + RIM, 0, SLOTS - 1)
-        for way, (across, along) in enumerate(((source, target), (target, source))):
-            line = [hc[d, pl.ds(along, 1), :] for d in range(3)]
-            for r in range(0, BS, 64):
-                col = [cbc[across, d, r : r + 64, :] for d in range(3)]
-                for h in range(2):
-                    dist = SOFT_SQ
-                    for d in range(3):
-                        diff = col[d] - line[d][:, 128 * h : 128 * h + 128]
-                        dist = dist + diff * diff
-                    tile = (NEAR_GAIN / BS) * lax.rsqrt(dist)
-                    high = tile.astype(BF16)
-                    tiles[k, way, 0, r : r + 64, 128 * h : 128 * h + 128] = high
-                    tiles[k, way, 1, r : r + 64, 128 * h : 128 * h + 128] = (tile - high.astype(F32)).astype(BF16)
+        target = jnp.clip(near_smem[1, k] - first, 0, BLK_DEV - 1)
+        line = [hc[d, pl.ds(source, 1), :] for d in range(3)]
+        for r in range(0, BS, 64):
+            col = [cbc[target, d, r : r + 64, :] for d in range(3)]
+            for h in range(2):
+                dist = SOFT_SQ
+                for d in range(3):
+                    diff = col[d] - line[d][:, 128 * h : 128 * h + 128]
+                    dist = dist + diff * diff
+                tile = (NEAR_GAIN / BS) * lax.rsqrt(dist)
+                high = tile.astype(BF16)
+                tiles[k, 0, r : r + 64, 128 * h : 128 * h + 128] = high
+                tiles[k, 1, r : r + 64, 128 * h : 128 * h + 128] = (tile - high.astype(F32)).astype(BF16)
         return 0
 
     give(0, b_own)
+    for d in range(3):
+        hct[pl.ds(BLK_DEV * d, BLK_DEV), :] = hc[d, RIM : RIM + BLK_DEV, :]
+    turned = hct[...].T
+    for b in range(BLK_DEV):
+        for d in range(3):
+            at = BLK_DEV * d + b
+            cbc[b, d] = jnp.broadcast_to(turned[:, at : at + 1], (BS, 128))
     pl.semaphore_wait(barrier, N_YZ - 1 + COLUMN - 1 + 2)
 
     for number, half, to in column:
@@ -354,9 +360,9 @@
     halo_down = send(
         hc.at[:, pl.ds(RIM, RIM)], hc.at[:, pl.ds(RIM + BLK_DEV, RIM)], once_sem.at[4], once_sem.at[5], down
     )
+    gather_start(0)
     halo_up.start()
     halo_down.start()
-    gather_start(0)
     span_start(0)
     wait_for(keys.at[pl.ds(0, COLUMN - 1)], once_sem.at[1], False)
     key = keys[0]
@@ -372,16 +378,9 @@
 
     halo_up.wait_recv()
     halo_down.wait_recv()
-    for d in range(3):
-        hct[pl.ds(SLOTS * d, SLOTS), :] = hc[d]
-    turned = hct[...].T
-    for b in range(SLOTS):
-        for d in range(3):
-            at = SLOTS * d + b
-            cbc[b, d] = jnp.broadcast_to(turned[:, at : at + 1], (BS, 128))
-    lax.fori_loop(0, NEAR_DEV // 4, build, 0)
+    lax.fori_loop(0, NEAR_DEV // 2, build, 0)
     gather_column(0, ((0, 0),))
-    lax.fori_loop(NEAR_DEV // 4, NEAR_DEV, build, 0)
+    lax.fori_loop(NEAR_DEV // 2, NEAR_DEV, build, 0)
     near(0)
     far_own, sums = gather_end(0)
     beta = jnp.sqrt(sums[0:1])
@@ -470,9 +469,9 @@
         pltpu.VMEM((1, FAR_DEV), jnp.int32),
         pltpu.VMEM((FAR_DEV, RMAX), F32),
         pltpu.VMEM((3, SLOTS, BS), F32),
-        pltpu.VMEM((3 * SLOTS, BS), F32),
-        pltpu.VMEM((SLOTS, 3, BS, 128), F32),
-        pltpu.VMEM((NEAR_DEV, 2, 2, BS, BS), BF16),
+        pltpu.VMEM((3 * BLK_DEV, BS), F32),
+        pltpu.VMEM((BLK_DEV, 3, BS, 128), F32),
+        pltpu.VMEM((NEAR_DEV, 2, BS, BS), BF16),
         pltpu.VMEM((COLUMN, 8, width), F32),
         pltpu.VMEM((ROWS, width), BF16),
         pltpu.VMEM((width, ROWS), BF16),

time: 66.9 us -> 64.8 us (0.969)
  Pallas kernels: 63 us -> 60.9 us
    pallas_call x1, Pallas kernels: 63 us -> 60.9 us  [body(): pl.pallas_call(kernel, out_shape=(jax.ShapeDtypeStruct((16, 128), F32), j...]
where the time goes in v4:
time: 64.8 us; the launch traced here: 64.6 us
  Pallas kernels  60.9 us (94%)
  between operations  2.41 us (4%)
  local copies, waits for them, and re-layouts  1.3 us (2%)
    pallas_call x1, Pallas kernels, body(): pl.pallas_call(kernel, out_shape=(jax.ShapeDtypeStruct((16, 128), F32), j...  60.9 us
    unnamed x1, local copies, waits for them, and re-layouts  1.3 us

profile of v4, /device:TPU:1, one launch (start us, length us, event | category | flops | bytes accessed | tf_op | source)
XLA Modules:
  0.0 64.6 jit_solution(3275908492404314916)
XLA Ops:
  0.6 60.9 %gmres.1 = (f32[16,128]{1,0:T(8,128)}, f32[1,1]{1,0:T(1,128)}) custom-call(s32[2,16]{1,0:T(2,128)} %near_hbm.1, f32[16,128]{1,0:T(8,128)} %bitcast.10, f32[3,2048]{1,0:T(4,128)} %coords_hbm.1, f32[16,128]{1,0:T(8,128)} %bitcast.11, s32[2,16]{1,0:T(2,128)} %near_hbm.1, s32[2,32]{1,0:T(2,128)} %far_hbm.1, s32[1,32]{1,0:T(1,128)} %bitcast.12, ...), custom_call_target="tpu_custom_call" | custom-call | flops 100000000 | bytes 2000000 | tf_op jit(solution)/shard_map/gmres/pallas_call | solution.py:498
  61.5 1.3 %copy.13 = f32[2048]{0:T(1024)} copy(f32[2048]{0:T(1024)} %bitcast.7) | data formatting | bytes 16384

commit v5 on v4

--- a/solution.py
+++ b/solution.py
@@ -83,7 +83,7 @@
     left, right, right_ref, coords_ref, diag_ref, near_ref, far_ref, rank_ref, scale_ref,
     hc, hct, cbc, tiles, keys, hot, hot_t, weight_d, hit_t,
     quarter, picked, got, given, taken, spread, landed, span, rim, joined,
-    rows_n, sums_yz, sums_c,
+    rows_n, shared, sums_yz,
     local_sem, once_sem, step_sem, sums_sem,
 ):
     x, y, z, core = place()
@@ -95,12 +95,13 @@
     mine = pl.ds(pl.multiple_of(yz * 4, 4), 4)
     up = {"patch": (patch + 1) % n_patch}
     down = {"patch": (patch + n_patch - 1) % n_patch}
-    x_peers = [device((x + i) % N_X, y, z, core) for i in range(1, N_X)]
     twin = device(x, y, z, 1 - core)
     column = []
     for i in (4, 5, 2, 3, 6, 7, 1):
         other_x, other_core = (x + i // 2) % N_X, (core + i) % 2
         column.append((2 * other_x + other_core, other_x % 2, device(other_x, y, z, other_core)))
+
+    joins = ([device((x + i) % N_X, y, z, core) for i in (2, 1, 3)], [to for _, _, to in column])
 
     barrier = pltpu.get_barrier_semaphore()
 
@@ -156,6 +157,8 @@
     b_own = natural(right_ref)
     diag = natural(diag_ref)
     span[0, RIM : RIM + BLK_DEV, :] = b_own
+    shared[core, 0] = b_own
+    shared[core, 1] = diag
     quarter[0, mine, :] = own_quarter(b_own)
     for d in range(3):
         for b in range(BLK_DEV):
@@ -306,14 +309,13 @@
         image = jnp.concatenate([image, image], axis=1)
         at_row = lax.broadcasted_iota(jnp.int32, (BLK_DEV, BS), 0) // 4
         at_half = lax.broadcasted_iota(jnp.int32, (BLK_DEV, BS), 1) // 128
-        joined[it, x] = local + jnp.where(2 * at_row + at_half == x, image, 0.0)
-        for i in (2, 1, 3):
-            send(
-                joined.at[it, x], joined.at[it, x], step_sem.at[it, 16], step_sem.at[it, 16 + i], x_peers[i - 1]
-            ).start()
-        for i in range(1, N_X):
-            wait_for(joined.at[it, (x + N_X - i) % N_X], step_sem.at[it, 16 + i], False)
-        return (joined[it, 0] + joined[it, 1]) + (joined[it, 2] + joined[it, 3])
+        joined[it, me] = local + jnp.where(2 * at_row + at_half == x, image, 0.0)
+        for to in joins[it]:
+            send(joined.at[it, me], joined.at[it, me], step_sem.at[it, 16], step_sem.at[it, 17], to).start()
+        wait_for(joined.at[it, pl.ds(0, len(joins[it]))], step_sem.at[it, 17], False)
+
+    def pair_sum(it, c):
+        return (joined[it, c] + joined[it, 2 + c]) + (joined[it, 4 + c] + joined[it, 6 + c])
 
     def sent(it):
         wait_for(taken.at[it, pl.ds(0, COLUMN - 1)], step_sem.at[it, 0], True)
@@ -324,7 +326,7 @@
         wait_for(got.at[it, pl.ds(0, COLUMN - 1)], step_sem.at[it, 10], True)
         wait_for(rim.at[it, 1, pl.ds(0, RIM)], step_sem.at[it, 12], True)
         wait_for(rim.at[it, 1, pl.ds(0, RIM)], step_sem.at[it, 14], True)
-        wait_for(joined.at[it, pl.ds(0, N_X - 1)], step_sem.at[it, 16], True)
+        wait_for(joined.at[it, pl.ds(0, len(joins[it]))], step_sem.at[it, 16], True)
 
     def build(k, _):
         source = jnp.clip(near_smem[0, k] - first + RIM, 0, SLOTS - 1)
@@ -364,6 +366,8 @@
     halo_up.start()
     halo_down.start()
     span_start(0)
+    constants = shared.at[core, pl.ds(0, 2)]
+    send(constants, constants, once_sem.at[6], once_sem.at[7], twin).start()
     wait_for(keys.at[pl.ds(0, COLUMN - 1)], once_sem.at[1], False)
     key = keys[0]
     for g in range(1, COLUMN):
@@ -385,7 +389,8 @@
     far_own, sums = gather_end(0)
     beta = jnp.sqrt(sums[0:1])
     inv_beta = 1.0 / beta
-    w_own = (join(0, far_own) + diag * b_own) * inv_beta
+    join(0, far_own)
+    w_own = (pair_sum(0, core) + diag * b_own) * inv_beta
 
     span[1, RIM : RIM + BLK_DEV, :] = w_own
     quarter[1, mine, :] = own_quarter(w_own)
@@ -393,6 +398,10 @@
     give_start(1)
     span_start(1)
     gather_start(1)
+    shared[core, 2] = w_own
+    krylov = shared.at[core, pl.ds(2, 1)]
+    send(krylov, krylov, once_sem.at[8], once_sem.at[9], twin).start()
+    wait_for(constants, once_sem.at[6], True)
     wait_for(keys.at[pl.ds(0, COLUMN - 1)], once_sem.at[0], True)
     halo_up.wait_send()
     halo_down.wait_send()
@@ -403,12 +412,19 @@
     far_own, sums = gather_end(1)
     h00 = sums[0:1] * inv_beta
     shift = sums[1:2] - h00 * h00
-    v0 = b_own * inv_beta
-    u = w_own - h00 * v0
-    rest = join(1, far_own) + diag * w_own - h00 * w_own - shift * v0 - h00 * u
+    alpha = h00 * inv_beta
+    wait_for(constants, once_sem.at[7], False)
+    wait_for(krylov, once_sem.at[9], False)
+    wait_for(krylov, once_sem.at[8], True)
+    v0 = shared[:, 0] * inv_beta
+    w = shared[:, 2]
+    u = w - h00 * v0
+    known = shared[:, 1] * w - h00 * w - shift * v0 - h00 * u
+    join(1, far_own)
+    rest = jnp.stack([pair_sum(1, c) for c in range(2)]) + known
 
     def lanes(value):
-        value = fold(value)
+        value = fold(value.reshape(2 * BLK_DEV, BS))
         return value[:, :128] + value[:, 128:]
 
     sums_yz[mine, :] = jnp.concatenate(
@@ -419,11 +435,7 @@
     sent(1)
     wait_for(sums_yz.at[pl.ds(0, ROWS - 4)], sums_sem.at[1], False)
     wait_for(sums_yz.at[pl.ds(0, ROWS - 4)], sums_sem.at[0], True)
-    sums_c[0] = jnp.sum(sums_yz[...].reshape(ROWS // 8, 8, 128), axis=0)
-    copy = send(sums_c.at[0], sums_c.at[1], sums_sem.at[2], sums_sem.at[3], twin)
-    copy.start()
-    copy.wait()
-    acc = sums_c[0] + sums_c[1]
+    acc = jnp.sum(sums_yz[...].reshape(ROWS // 8, 8, 128), axis=0)
     acc = jnp.sum(acc[:4] + acc[4:], axis=1, keepdims=True)
     sq, a0, a1, uu = acc[0:1], acc[1:2], acc[2:3], acc[3:4]
     h10 = jnp.sqrt(uu)
@@ -446,7 +458,8 @@
     y1 = c1 * g1 / rho1
     y0 = (g0 - r01 * y1) / rho0
     norm_ref[...] = jnp.abs(s1 * g1)
-    answer = y0 * v0 + (y1 * inv_h10) * u
+    u_own = w_own - alpha * b_own
+    answer = (y0 * inv_beta) * b_own + (y1 * inv_h10) * u_own
     for h in range(2):
         out_ref[pl.ds(h, BLK_DEV, stride=2), :] = answer[:, 128 * h : 128 * h + 128]
 
@@ -486,14 +499,14 @@
         pltpu.VMEM((2, ROWS, 128), F32),
         pltpu.VMEM((2, SLOTS, BS), F32),
         pltpu.VMEM((2, 2, SLOTS, BS), F32),
-        pltpu.VMEM((2, N_X, BLK_DEV, BS), F32),
+        pltpu.VMEM((2, COLUMN, BLK_DEV, BS), F32),
         pltpu.VMEM((2 * NEAR_DEV, BS), F32),
+        pltpu.VMEM((2, 3, BLK_DEV, BS), F32),
         pltpu.VMEM((ROWS, 128), F32),
-        pltpu.VMEM((2, 8, 128), F32),
         pltpu.SemaphoreType.DMA((9,)),
-        pltpu.SemaphoreType.DMA((6,)),
-        pltpu.SemaphoreType.DMA((2, 20)),
-        pltpu.SemaphoreType.DMA((4,)),
+        pltpu.SemaphoreType.DMA((10,)),
+        pltpu.SemaphoreType.DMA((2, 18)),
+        pltpu.SemaphoreType.DMA((2,)),
     ]
     solution, norm = pl.pallas_call(
         kernel,

time: 64.8 us -> 63.1 us (0.974)
  Pallas kernels: 60.9 us -> 59.2 us
    pallas_call x1, Pallas kernels: 60.9 us -> 59.2 us  [body(): pl.pallas_call(kernel, out_shape=(jax.ShapeDtypeStruct((16, 128), F32), j...]
where the time goes in v5:
time: 63.1 us; the launch traced here: 62.9 us
  Pallas kernels  59.2 us (94%)
  between operations  2.41 us (4%)
  local copies, waits for them, and re-layouts  1.3 us (2%)
    pallas_call x1, Pallas kernels, body(): pl.pallas_call(kernel, out_shape=(jax.ShapeDtypeStruct((16, 128), F32), j...  59.2 us
    unnamed x1, local copies, waits for them, and re-layouts  1.3 us

profile of v5, /device:TPU:1, one launch (start us, length us, event | category | flops | bytes accessed | tf_op | source)
XLA Modules:
  0.0 62.9 jit_solution(15383652999278126190)
XLA Ops:
  0.6 59.2 %gmres.1 = (f32[16,128]{1,0:T(8,128)}, f32[1,1]{1,0:T(1,128)}) custom-call(s32[2,16]{1,0:T(2,128)} %near_hbm.1, f32[16,128]{1,0:T(8,128)} %bitcast.10, f32[3,2048]{1,0:T(4,128)} %coords_hbm.1, f32[16,128]{1,0:T(8,128)} %bitcast.11, s32[2,16]{1,0:T(2,128)} %near_hbm.1, s32[2,32]{1,0:T(2,128)} %far_hbm.1, s32[1,32]{1,0:T(1,128)} %bitcast.12, ...), custom_call_target="tpu_custom_call" | custom-call | flops 100000000 | bytes 2000000 | tf_op jit(solution)/shard_map/gmres/pallas_call | solution.py:511
  59.8 1.3 %copy.13 = f32[2048]{0:T(1024)} copy(f32[2048]{0:T(1024)} %bitcast.7) | data formatting | bytes 16384

commit v6 on v5

--- a/solution.py
+++ b/solution.py
@@ -82,7 +82,7 @@
     out_ref, norm_ref,
     left, right, right_ref, coords_ref, diag_ref, near_ref, far_ref, rank_ref, scale_ref,
     hc, hct, cbc, tiles, keys, hot, hot_t, weight_d, hit_t,
-    quarter, picked, got, given, taken, spread, landed, span, rim, joined,
+    quarter, picked, got, given, taken, spread, landed, span, rim, rim_in, joined,
     rows_n, shared, sums_yz,
     local_sem, once_sem, step_sem, sums_sem,
 ):
@@ -93,8 +93,9 @@
     yz = y * N_Z + z
     me = 2 * x + core
     mine = pl.ds(pl.multiple_of(yz * 4, 4), 4)
-    up = {"patch": (patch + 1) % n_patch}
-    down = {"patch": (patch + n_patch - 1) % n_patch}
+    up = {"patch": (patch + 1) % n_patch, "pair": x}
+    down = {"patch": (patch + n_patch - 1) % n_patch, "pair": x}
+    rims = ([(x + i) % N_X for i in range(N_X)], [x])
     twin = device(x, y, z, 1 - core)
     column = []
     for i in (4, 5, 2, 3, 6, 7, 1):
@@ -107,17 +108,18 @@
 
     z_peers = [((z + d) % N_Z, d) for d in far_first(N_Z)]
 
-    def over_plane(act):
+    def over_plane(act, begin=0, end=N_Y):
         def rows(k, _):
             other_y = (y + N_Y // 2 + ((k + 1) // 2) * (1 - 2 * (k % 2))) % N_Y
             for other_z, _ in z_peers:
                 act(other_y, other_z)
             return 0
 
-        lax.fori_loop(0, N_Y - 1, rows, 0)
-        for other_z, d in z_peers:
-            if d:
-                act(y, other_z)
+        lax.fori_loop(begin, min(end, N_Y - 1), rows, 0)
+        if end == N_Y:
+            for other_z, d in z_peers:
+                if d:
+                    act(y, other_z)
 
     def greet(other_y, other_z):
         pl.semaphore_signal(
@@ -127,8 +129,11 @@
     over_plane(greet)
     for _, _, to in column:
         pl.semaphore_signal(barrier, inc=1, device_id=to, device_id_type=MESH)
-    for to in (up, down):
-        pl.semaphore_signal(barrier, inc=1, device_id=to, device_id_type=MESH)
+    for other in rims[0]:
+        for to in (up, down):
+            pl.semaphore_signal(
+                barrier, inc=1, device_id={"patch": to["patch"], "pair": other}, device_id_type=MESH
+            )
     loads = [
         pltpu.make_async_copy(src, dst, local_sem.at[i])
         for i, (src, dst) in enumerate(
@@ -194,12 +199,12 @@
         else:
             copy.wait_recv()
 
-    def plane(step, sems):
+    def plane(step, sems, begin=0, end=N_Y):
         def each(other_y, other_z):
             src, dst = step(other_y * N_Z + other_z)
             send(src, dst, sems[0], sems[1], device(x, other_y, other_z, core)).start()
 
-        over_plane(each)
+        over_plane(each, begin, end)
 
     def give(it, own_value):
         back = dot_rows(split(own_value), left[...])
@@ -214,9 +219,9 @@
         for number, half, to in column:
             send(given.at[it, half], taken.at[it, me], step_sem.at[it, 0], step_sem.at[it, 1], to).start()
 
-    def gather_start(it):
+    def gather_start(it, begin, end):
         own_rows = quarter.at[it, mine]
-        plane(lambda there: (own_rows, own_rows), (step_sem.at[it, 2], step_sem.at[it, 3]))
+        plane(lambda there: (own_rows, own_rows), (step_sem.at[it, 2], step_sem.at[it, 3]), begin, end)
 
     def span_start(it):
         send(
@@ -231,7 +236,7 @@
     def scatter_plane(it):
         wait_for(taken.at[it, pl.ds(0, COLUMN - 1)], step_sem.at[it, 1], False)
         value = 0.0
-        for part in parts(taken[it].reshape(COLUMN * FAR_DEV, 128), 3):
+        for part in parts(taken[it].reshape(COLUMN * FAR_DEV, 128), 2):
             value = value + dot(hot[...], part)
         spread[it] = value
         landed[it, mine, :] = spread[it, mine, :]
@@ -243,7 +248,7 @@
     def gather_column(it, extras):
         wait_for(quarter.at[it, pl.ds(0, ROWS - 4)], step_sem.at[it, 3], False)
         value = 0.0
-        for part in parts(quarter[it], 3):
+        for part in parts(quarter[it], 2):
             value = value + dot(hot_t[...], part)
         picked[it, :, pl.ds(0, FAR_DEV), :] = value.reshape(COLUMN, FAR_DEV, 128)
         sums = [fold(quarter[i] * quarter[j]) for i, j in extras]
@@ -288,20 +293,26 @@
         value = 0.0
         for part in parts(rows_n[...], 3):
             value = value + dot(hits, part)
-        rim[it, 0] = value
-        send(
-            rim.at[it, 0, pl.ds(0, RIM)], rim.at[it, 1, pl.ds(RIM, RIM)],
-            step_sem.at[it, 12], step_sem.at[it, 13], down,
-        ).start()
-        send(
-            rim.at[it, 0, pl.ds(RIM + BLK_DEV, RIM)], rim.at[it, 1, pl.ds(0, RIM)],
-            step_sem.at[it, 14], step_sem.at[it, 15], up,
-        ).start()
+        rim[it] = value
+        for other in rims[it]:
+            send(
+                rim.at[it, pl.ds(0, RIM)], rim_in.at[it, x, pl.ds(RIM, RIM)],
+                step_sem.at[it, 12], step_sem.at[it, 13], {"patch": down["patch"], "pair": other},
+            ).start()
+            send(
+                rim.at[it, pl.ds(RIM + BLK_DEV, RIM)], rim_in.at[it, x, pl.ds(0, RIM)],
+                step_sem.at[it, 14], step_sem.at[it, 15], {"patch": up["patch"], "pair": other},
+            ).start()
+
+    def rim_wait(it, at, sent):
+        wait_for(rim.at[it, pl.ds(0, RIM * len(rims[it]))], step_sem.at[it, at], sent)
 
     def join(it, far_own):
-        wait_for(rim.at[it, 1, pl.ds(0, RIM)], step_sem.at[it, 13], False)
-        wait_for(rim.at[it, 1, pl.ds(0, RIM)], step_sem.at[it, 15], False)
-        local = far_own + rim[it, 0, RIM : RIM + BLK_DEV, :] + rim[it, 1, 0:BLK_DEV, :]
+        local = far_own + rim[it, RIM : RIM + BLK_DEV, :]
+        if len(rims[it]) == 1:
+            rim_wait(it, 13, False)
+            rim_wait(it, 15, False)
+            local = local + rim_in[it, x]
         wait_for(landed.at[it, pl.ds(0, ROWS - 4)], step_sem.at[it, 9], False)
         image = jnp.sum(landed[it].reshape(ROWS // 8, 8, 128), axis=0)
         image = image[:4] + image[4:]
@@ -324,8 +335,8 @@
         wait_for(span.at[it, pl.ds(0, RIM)], step_sem.at[it, 6], True)
         wait_for(landed.at[it, pl.ds(0, ROWS - 4)], step_sem.at[it, 8], True)
         wait_for(got.at[it, pl.ds(0, COLUMN - 1)], step_sem.at[it, 10], True)
-        wait_for(rim.at[it, 1, pl.ds(0, RIM)], step_sem.at[it, 12], True)
-        wait_for(rim.at[it, 1, pl.ds(0, RIM)], step_sem.at[it, 14], True)
+        rim_wait(it, 12, True)
+        rim_wait(it, 14, True)
         wait_for(joined.at[it, pl.ds(0, len(joins[it]))], step_sem.at[it, 16], True)
 
     def build(k, _):
@@ -353,8 +364,9 @@
         for d in range(3):
             at = BLK_DEV * d + b
             cbc[b, d] = jnp.broadcast_to(turned[:, at : at + 1], (BS, 128))
-    pl.semaphore_wait(barrier, N_YZ - 1 + COLUMN - 1 + 2)
-
+    pl.semaphore_wait(barrier, N_YZ - 1 + COLUMN - 1 + 2 * N_X)
+
+    gather_start(0, 0, 2)
     for number, half, to in column:
         send(keys.at[me], keys.at[me], once_sem.at[0], once_sem.at[1], to).start()
     give_start(0)
@@ -362,12 +374,15 @@
     halo_down = send(
         hc.at[:, pl.ds(RIM, RIM)], hc.at[:, pl.ds(RIM + BLK_DEV, RIM)], once_sem.at[4], once_sem.at[5], down
     )
-    gather_start(0)
     halo_up.start()
     halo_down.start()
+    gather_start(0, 2, N_Y)
     span_start(0)
     constants = shared.at[core, pl.ds(0, 2)]
     send(constants, constants, once_sem.at[6], once_sem.at[7], twin).start()
+    halo_up.wait_recv()
+    halo_down.wait_recv()
+    lax.fori_loop(0, 8, build, 0)
     wait_for(keys.at[pl.ds(0, COLUMN - 1)], once_sem.at[1], False)
     key = keys[0]
     for g in range(1, COLUMN):
@@ -380,24 +395,26 @@
     hot_t[...] = hits.T.astype(BF16)
     scatter_plane(0)
 
-    halo_up.wait_recv()
-    halo_down.wait_recv()
-    lax.fori_loop(0, NEAR_DEV // 2, build, 0)
+    lax.fori_loop(8, 14, build, 0)
     gather_column(0, ((0, 0),))
-    lax.fori_loop(NEAR_DEV // 2, NEAR_DEV, build, 0)
+    lax.fori_loop(14, NEAR_DEV, build, 0)
     near(0)
     far_own, sums = gather_end(0)
     beta = jnp.sqrt(sums[0:1])
     inv_beta = 1.0 / beta
     join(0, far_own)
-    w_own = (pair_sum(0, core) + diag * b_own) * inv_beta
+    rim_wait(0, 13, False)
+    rim_wait(0, 15, False)
+    from_rims = (rim_in[0, 0] + rim_in[0, 1]) + (rim_in[0, 2] + rim_in[0, 3])
+    w_own = (pair_sum(0, core) + from_rims + diag * b_own) * inv_beta
 
     span[1, RIM : RIM + BLK_DEV, :] = w_own
     quarter[1, mine, :] = own_quarter(w_own)
+    gather_start(1, 0, 2)
     give(1, w_own)
     give_start(1)
+    gather_start(1, 2, N_Y)
     span_start(1)
-    gather_start(1)
     shared[core, 2] = w_own
     krylov = shared.at[core, pl.ds(2, 1)]
     send(krylov, krylov, once_sem.at[8], once_sem.at[9], twin).start()
@@ -498,7 +515,8 @@
         pltpu.VMEM((2, ROWS, 128), F32),
         pltpu.VMEM((2, ROWS, 128), F32),
         pltpu.VMEM((2, SLOTS, BS), F32),
-        pltpu.VMEM((2, 2, SLOTS, BS), F32),
+        pltpu.VMEM((2, SLOTS, BS), F32),
+        pltpu.VMEM((2, N_X, BLK_DEV, BS), F32),
         pltpu.VMEM((2, COLUMN, BLK_DEV, BS), F32),
         pltpu.VMEM((2 * NEAR_DEV, BS), F32),
         pltpu.VMEM((2, 3, BLK_DEV, BS), F32),

time: 63.1 us -> 61.9 us (0.981)
  Pallas kernels: 59.2 us -> 57.9 us
    pallas_call x1, Pallas kernels: 59.2 us -> 57.9 us  [body(): pl.pallas_call(kernel, out_shape=(jax.ShapeDtypeStruct((16, 128), F32), j...]
where the time goes in v6:
time: 61.9 us; the launch traced here: 61.6 us
  Pallas kernels  57.9 us (94%)
  between operations  2.41 us (4%)
  local copies, waits for them, and re-layouts  1.3 us (2%)
    pallas_call x1, Pallas kernels, body(): pl.pallas_call(kernel, out_shape=(jax.ShapeDtypeStruct((16, 128), F32), j...  57.9 us
    unnamed x1, local copies, waits for them, and re-layouts  1.3 us

profile of v6, /device:TPU:1, one launch (start us, length us, event | category | flops | bytes accessed | tf_op | source)
XLA Modules:
  0.0 61.6 jit_solution(4409400054056838425)
XLA Ops:
  0.6 57.9 %gmres.1 = (f32[16,128]{1,0:T(8,128)}, f32[1,1]{1,0:T(1,128)}) custom-call(s32[2,16]{1,0:T(2,128)} %near_hbm.1, f32[16,128]{1,0:T(8,128)} %bitcast.10, f32[3,2048]{1,0:T(4,128)} %coords_hbm.1, f32[16,128]{1,0:T(8,128)} %bitcast.11, s32[2,16]{1,0:T(2,128)} %near_hbm.1, s32[2,32]{1,0:T(2,128)} %far_hbm.1, s32[1,32]{1,0:T(1,128)} %bitcast.12, ...), custom_call_target="tpu_custom_call" | custom-call | flops 100000000 | bytes 2000000 | tf_op jit(solution)/shard_map/gmres/pallas_call | solution.py:529
  58.6 1.3 %copy.13 = f32[2048]{0:T(1024)} copy(f32[2048]{0:T(1024)} %bitcast.7) | data formatting | bytes 16384

commit v7 on v6

--- a/solution.py
+++ b/solution.py
@@ -80,7 +80,7 @@
 def kernel(
     near_smem, right_hbm, coords_hbm, diag_hbm, near_hbm, far_hbm, rank_hbm, scale_hbm, left_hbm, factor_hbm,
     out_ref, norm_ref,
-    left, right, right_ref, coords_ref, diag_ref, near_ref, far_ref, rank_ref, scale_ref,
+    left, right, left_t, right_t, right_ref, coords_ref, diag_ref, near_ref, far_ref, rank_ref, scale_ref,
     hc, hct, cbc, tiles, keys, hot, hot_t, weight_d, hit_t,
     quarter, picked, got, given, taken, spread, landed, span, rim, rim_in, joined,
     rows_n, shared, sums_yz,
@@ -207,7 +207,7 @@
         over_plane(each, begin, end)
 
     def give(it, own_value):
-        back = dot_rows(split(own_value), left[...])
+        back = dot(split(own_value), left_t[...])
         back = fold(hit_t[...] * (back[:BLK_DEV] + back[BLK_DEV:]))
         to_far = dot(split(weight_d[...] * back), right[...])
         to_far = to_far[:FAR_DEV] + to_far[FAR_DEV:]
@@ -267,7 +267,7 @@
             halves.append((got[it, at] + got[it, at + 1]) + (got[it, at + 4] + got[it, at + 5]))
         sums = jnp.sum(halves[0][FAR_DEV:] + halves[1][FAR_DEV:], axis=1, keepdims=True)
         far_v = split(jnp.concatenate([half[:FAR_DEV] for half in halves], axis=1))
-        coef = dot_rows(far_v, right[...])
+        coef = dot(far_v, right_t[...])
         coef = fold(weight_d[...] * (coef[:FAR_DEV] + coef[FAR_DEV:]))
         to_own = dot(split(hit_t[...] * coef), left[...])
         return to_own[:BLK_DEV] + to_own[BLK_DEV:], sums
@@ -356,6 +356,8 @@
                 tiles[k, 1, r : r + 64, 128 * h : 128 * h + 128] = (tile - high.astype(F32)).astype(BF16)
         return 0
 
+    left_t[...] = left[...].T
+    right_t[...] = right[...].T
     give(0, b_own)
     for d in range(3):
         hct[pl.ds(BLK_DEV * d, BLK_DEV), :] = hc[d, RIM : RIM + BLK_DEV, :]
@@ -366,7 +368,7 @@
             cbc[b, d] = jnp.broadcast_to(turned[:, at : at + 1], (BS, 128))
     pl.semaphore_wait(barrier, N_YZ - 1 + COLUMN - 1 + 2 * N_X)
 
-    gather_start(0, 0, 2)
+    gather_start(0, 0, 1)
     for number, half, to in column:
         send(keys.at[me], keys.at[me], once_sem.at[0], once_sem.at[1], to).start()
     give_start(0)
@@ -376,7 +378,7 @@
     )
     halo_up.start()
     halo_down.start()
-    gather_start(0, 2, N_Y)
+    gather_start(0, 1, N_Y)
     span_start(0)
     constants = shared.at[core, pl.ds(0, 2)]
     send(constants, constants, once_sem.at[6], once_sem.at[7], twin).start()
@@ -410,10 +412,10 @@
 
     span[1, RIM : RIM + BLK_DEV, :] = w_own
     quarter[1, mine, :] = own_quarter(w_own)
-    gather_start(1, 0, 2)
+    gather_start(1, 0, 1)
     give(1, w_own)
     give_start(1)
-    gather_start(1, 2, N_Y)
+    gather_start(1, 1, N_Y)
     span_start(1)
     shared[core, 2] = w_own
     krylov = shared.at[core, pl.ds(2, 1)]
@@ -491,6 +493,8 @@
     scratch = [
         pltpu.VMEM((FACT, BS), BF16),
         pltpu.VMEM((FACT, BS), BF16),
+        pltpu.VMEM((BS, FACT), BF16),
+        pltpu.VMEM((BS, FACT), BF16),
         pltpu.VMEM((16, 128), F32),
         pltpu.VMEM((3, BLK_DEV * BS), F32),
         pltpu.VMEM((16, 128), F32),

time: 61.9 us -> 61.9 us (level)
  no operation moved by 1% of the time
where the time goes in v7:
time: 61.9 us; the launch traced here: 61.5 us
  Pallas kernels  57.8 us (93%)
  between operations  2.41 us (4%)
  local copies, waits for them, and re-layouts  1.3 us (2%)
    pallas_call x1, Pallas kernels, body(): pl.pallas_call(kernel, out_shape=(jax.ShapeDtypeStruct((16, 128), F32), j...  57.8 us
    unnamed x1, local copies, waits for them, and re-layouts  1.3 us

profile of v7, /device:TPU:1, one launch (start us, length us, event | category | flops | bytes accessed | tf_op | source)
XLA Modules:
  0.0 61.5 jit_solution(4657283747828572808)
XLA Ops:
  0.6 57.8 %gmres.1 = (f32[16,128]{1,0:T(8,128)}, f32[1,1]{1,0:T(1,128)}) custom-call(s32[2,16]{1,0:T(2,128)} %near_hbm.1, f32[16,128]{1,0:T(8,128)} %bitcast.10, f32[3,2048]{1,0:T(4,128)} %coords_hbm.1, f32[16,128]{1,0:T(8,128)} %bitcast.11, s32[2,16]{1,0:T(2,128)} %near_hbm.1, s32[2,32]{1,0:T(2,128)} %far_hbm.1, s32[1,32]{1,0:T(1,128)} %bitcast.12, ...), custom_call_target="tpu_custom_call" | custom-call | flops 100000000 | bytes 2000000 | tf_op jit(solution)/shard_map/gmres/pallas_call | solution.py:533
  58.5 1.3 %copy.13 = f32[2048]{0:T(1024)} copy(f32[2048]{0:T(1024)} %bitcast.7) | data formatting | bytes 16384

commit v8 on v7

--- a/solution.py
+++ b/solution.py
@@ -175,7 +175,7 @@
     lane_key = lax.broadcasted_iota(jnp.int32, (FAR_DEV, COLUMN * FAR_DEV), 1)
     pick = (lane_key == sub_key + me * FAR_DEV).astype(F32)
     laid = jnp.dot(far_f, pick, precision=HIGH, preferred_element_type=F32)
-    keys[me] = jnp.broadcast_to(laid[0:1], (8, COLUMN * FAR_DEV))
+    keys[me] = laid[0:1]
 
     pair_of = lax.broadcasted_iota(jnp.int32, (FAR_DEV, FACT), 1) // RMAX
     term_of = lax.broadcasted_iota(jnp.int32, (FAR_DEV, FACT), 1) % RMAX
@@ -389,13 +389,13 @@
     key = keys[0]
     for g in range(1, COLUMN):
         key = key + keys[g]
-    key = (key[0:1] + 0.5).astype(jnp.int32)
+    key = (key + 0.5).astype(jnp.int32)
     row = lax.broadcasted_iota(jnp.int32, (ROWS, COLUMN * FAR_DEV), 0)
     block = (row // 4) * 16 + core * 8 + (x // 2) * 4 + row % 4
     hits = (block == key).astype(F32)
     hot[...] = hits.astype(BF16)
+    scatter_plane(0)
     hot_t[...] = hits.T.astype(BF16)
-    scatter_plane(0)
 
     lax.fori_loop(8, 14, build, 0)
     gather_column(0, ((0, 0),))
@@ -506,7 +506,7 @@
         pltpu.VMEM((3 * BLK_DEV, BS), F32),
         pltpu.VMEM((BLK_DEV, 3, BS, 128), F32),
         pltpu.VMEM((NEAR_DEV, 2, BS, BS), BF16),
-        pltpu.VMEM((COLUMN, 8, width), F32),
+        pltpu.VMEM((COLUMN, 1, width), F32),
         pltpu.VMEM((ROWS, width), BF16),
         pltpu.VMEM((width, ROWS), BF16),
         pltpu.VMEM((FAR_DEV, FACT), F32),

time: 61.9 us -> 62 us (level)
  no operation moved by 1% of the time
where the time goes in v8:
time: 62 us; the launch traced here: 61.7 us
  Pallas kernels  58 us (94%)
  between operations  2.41 us (4%)
  local copies, waits for them, and re-layouts  1.3 us (2%)
    pallas_call x1, Pallas kernels, body(): pl.pallas_call(kernel, out_shape=(jax.ShapeDtypeStruct((16, 128), F32), j...  58 us
    unnamed x1, local copies, waits for them, and re-layouts  1.3 us

profile of v8, /device:TPU:1, one launch (start us, length us, event | category | flops | bytes accessed | tf_op | source)
XLA Modules:
  0.0 61.7 jit_solution(4932004718440020750)
XLA Ops:
  0.6 58.0 %gmres.1 = (f32[16,128]{1,0:T(8,128)}, f32[1,1]{1,0:T(1,128)}) custom-call(s32[2,16]{1,0:T(2,128)} %near_hbm.1, f32[16,128]{1,0:T(8,128)} %bitcast.10, f32[3,2048]{1,0:T(4,128)} %coords_hbm.1, f32[16,128]{1,0:T(8,128)} %bitcast.11, s32[2,16]{1,0:T(2,128)} %near_hbm.1, s32[2,32]{1,0:T(2,128)} %far_hbm.1, s32[1,32]{1,0:T(1,128)} %bitcast.12, ...), custom_call_target="tpu_custom_call" | custom-call | flops 100000000 | bytes 2000000 | tf_op jit(solution)/shard_map/gmres/pallas_call | solution.py:533
  58.7 1.3 %copy.13 = f32[2048]{0:T(1024)} copy(f32[2048]{0:T(1024)} %bitcast.7) | data formatting | bytes 16384
